TPU v7x, 256 devices: a whole 4x4x8 slice. The times are simulated.
256 devices in a mesh: seq: 16 (over z, core), exp: 16 (over y, x).
Axes of the slice: x: 4, y: 4, z: 8, core: 2. Of those that a mesh axis runs over, the one named last changes fastest.
Arguments:
- queries: bfloat16 [16, 2048, 4096], P('exp', 'seq'), may hold values from -65 to 65
- keys: bfloat16 [16, 2048, 256], P('exp', 'seq'), may hold values from -5 to 5
- values: bfloat16 [16, 2048, 256], P('exp', 'seq'), may hold values from -6 to 6
- attn_out: bfloat16 [16, 2048, 4096], P('exp', 'seq'), may hold values from -6 to 6
- d_attn: bfloat16 [16, 2048, 4096], P('exp', 'seq'), may hold values from -6 to 6
- normed: bfloat16 [16, 2048, 2048], P('exp', 'seq'), may hold values from -6 to 6
- d_moe: bfloat16 [16, 2048, 2048], P('exp', 'seq'), may hold values from -6 to 6
- expert_ids: int32 [16, 2048, 8], P('exp', 'seq'), may hold values from 0 to 127, all different within a row; in each aligned block of 128 rows (0 to 127, 128 to 255, ..., all dimensions but the last counted through in order) at most 10 rows name the same one
- route_weight: float32 [16, 2048, 8], P('exp', 'seq'), may hold values from 0.05 to 0.5
- gate_w: bfloat16 [16, 2048, 1536], P('exp', 'seq'), may hold values from -0.125 to 0.125
- up_w: bfloat16 [16, 2048, 1536], P('exp', 'seq'), may hold values from -0.125 to 0.125
- down_t: bfloat16 [16, 2048, 1536], P('exp', 'seq'), may hold values from -0.15625 to 0.15625
Outputs:
- d_queries: bfloat16 [16, 2048, 4096], P('exp', 'seq')
- key_gradient: bfloat16 [16, 2048, 256], P('exp', 'seq')
- value_gradient: bfloat16 [16, 2048, 256], P('exp', 'seq')
- d_normed: bfloat16 [16, 2048, 2048], P('exp', 'seq')
Inputs may be any that keep to these rules, and one draw needn't show every extreme that they name: `expert_ids`: in the 128 rows of one device no expert is named more than 10 times, a bound that some block reaches.
All inputs are finite; a program needn't handle non-finite values.
Results may differ from a plain program's by a relative error of at most 0.0057.
Values may be sent and summed in bfloat16 or wider, within the bound.
A program may use at most 192 MiB of HBM per device.

v0:
```python
import math

import jax
import jax.numpy as jnp
from jax import lax
from jax.sharding import PartitionSpec as P

D = 2048
QUERY_HEADS = 32
KEY_VALUE_HEADS = 2
HEAD_SIZE = 128
TOPK = 8
CAP = 10


def head_gradients(query_heads, key_heads, value_heads, output_heads, grad_heads):
    head_count, length, head_width = query_heads.shape
    shared = key_heads.shape[0] == 1
    scaling = 1.0 / math.sqrt(head_width)
    block_size = min(512, length)
    query_parts = []
    key_grad = jnp.zeros(key_heads.shape, jnp.float32)
    value_grad = jnp.zeros(value_heads.shape, jnp.float32)
    row_dot = jnp.sum(grad_heads.astype(jnp.float32) * output_heads.astype(jnp.float32), axis=-1)
    for start_row in range(0, length, block_size):
        stop_row = start_row + block_size
        query_block = query_heads[:, start_row:stop_row]
        grad_block = grad_heads[:, start_row:stop_row]
        key_block = key_heads[:, :stop_row]
        value_block = value_heads[:, :stop_row]
        scores = (
            jnp.einsum("hqd,hkd->hqk", query_block, key_block, preferred_element_type=jnp.float32)
            * scaling
        )
        grad_weights = jnp.einsum(
            "hqd,hkd->hqk", grad_block, value_block, preferred_element_type=jnp.float32
        )
        row_pos = start_row + jnp.arange(block_size, dtype=jnp.int32)[:, None]
        col_pos = jnp.arange(stop_row, dtype=jnp.int32)[None, :]
        scores = jnp.where(col_pos <= row_pos, scores, -jnp.inf)
        row_max = jnp.max(scores, axis=-1, keepdims=True)
        log_total = row_max + jnp.log(jnp.sum(jnp.exp(scores - row_max), axis=-1, keepdims=True))
        weights = jnp.exp(scores - log_total)
        weights_low = weights.astype(jnp.bfloat16)
        grad_scores = (weights * (grad_weights - row_dot[:, start_row:stop_row, None])).astype(
            jnp.bfloat16
        )
        query_part = jnp.einsum(
            "hqk,hkd->hqd", grad_scores, key_block, preferred_element_type=jnp.float32
        )
        key_piece = jnp.einsum(
            "hqk,hqd->hkd", grad_scores, query_block, preferred_element_type=jnp.float32
        )
        value_piece = jnp.einsum(
            "hqk,hqd->hkd", weights_low, grad_block, preferred_element_type=jnp.float32
        )
        query_parts.append((query_part * scaling).astype(jnp.bfloat16))
        key_grad = key_grad.at[:, :stop_row].add(key_piece * scaling)
        value_grad = value_grad.at[:, :stop_row].add(value_piece)
    return (jnp.concatenate(query_parts, axis=1), key_grad, value_grad)


def activation_grads(gate_val, up_val, hidden_grad):
    sigmoid = jax.nn.sigmoid(gate_val)
    activated = gate_val * sigmoid
    gate_grad = (hidden_grad * up_val * sigmoid * (1.0 + gate_val * (1.0 - sigmoid))).astype(
        jnp.bfloat16
    )
    up_grad = (hidden_grad * activated).astype(jnp.bfloat16)
    return (gate_grad, up_grad)


def back_columns(gate_grad, up_grad, gate_piece, up_piece):
    contract = (((1,), (1,)), ((), ()))
    return lax.dot_general(
        gate_grad, gate_piece, contract, preferred_element_type=jnp.float32
    ) + lax.dot_general(up_grad, up_piece, contract, preferred_element_type=jnp.float32)


def heads_first(arrived, length, head_count):
    return jnp.transpose(arrived.reshape(length, head_count, HEAD_SIZE), (1, 0, 2))


def tokens_first(head_major, length):
    return jnp.transpose(head_major, (1, 0, 2)).reshape(length, 1, head_major.shape[0] * HEAD_SIZE)


def local(
    queries,
    keys,
    values,
    attn_out,
    d_attn,
    normed,
    d_moe,
    expert_ids,
    route_weight,
    gate_w,
    up_w,
    down_t,
):
    seq_count = lax.axis_size("seq")
    token_row_block = queries.shape[1]
    length = token_row_block * seq_count
    heads_dev = QUERY_HEADS // seq_count
    query_group_width = QUERY_HEADS // KEY_VALUE_HEADS
    slot_width = heads_dev * HEAD_SIZE
    query_in, output_in, grad_in = (
        lax.all_to_all(
            queries[0].reshape(token_row_block, seq_count, slot_width),
            "seq",
            split_axis=1,
            concat_axis=0,
            tiled=True,
        ),
        lax.all_to_all(
            attn_out[0].reshape(token_row_block, seq_count, slot_width),
            "seq",
            split_axis=1,
            concat_axis=0,
            tiled=True,
        ),
        lax.all_to_all(
            d_attn[0].reshape(token_row_block, seq_count, slot_width),
            "seq",
            split_axis=1,
            concat_axis=0,
            tiled=True,
        ),
    )
    query_heads = heads_first(query_in, length, heads_dev)
    output_heads = heads_first(output_in, length, heads_dev)
    grad_heads = heads_first(grad_in, length, heads_dev)
    resident_keys = keys[0].reshape(token_row_block, KEY_VALUE_HEADS, HEAD_SIZE)
    resident_values = values[0].reshape(token_row_block, KEY_VALUE_HEADS, HEAD_SIZE)
    key_send = jnp.repeat(resident_keys, query_group_width, axis=1).reshape(
        token_row_block, seq_count, slot_width
    )
    value_send = jnp.repeat(resident_values, query_group_width, axis=1).reshape(
        token_row_block, seq_count, slot_width
    )
    key_in, value_in = (
        lax.all_to_all(key_send, "seq", split_axis=1, concat_axis=0, tiled=True),
        lax.all_to_all(value_send, "seq", split_axis=1, concat_axis=0, tiled=True),
    )
    grad_q, key_gradient_part, value_gradient_part = head_gradients(
        query_heads,
        heads_first(key_in, length, heads_dev),
        heads_first(value_in, length, heads_dev),
        output_heads,
        grad_heads,
    )
    backward_keys, backward_values = (
        lax.all_to_all(
            tokens_first(key_gradient_part, length), "seq", split_axis=0, concat_axis=1, tiled=True
        ),
        lax.all_to_all(
            tokens_first(value_gradient_part, length),
            "seq",
            split_axis=0,
            concat_axis=1,
            tiled=True,
        ),
    )
    key_gradient_sum = backward_keys.reshape(
        token_row_block, KEY_VALUE_HEADS, query_group_width, HEAD_SIZE
    ).sum(2)
    value_gradient_sum = backward_values.reshape(
        token_row_block, KEY_VALUE_HEADS, query_group_width, HEAD_SIZE
    ).sum(2)
    query_back = lax.all_to_all(
        tokens_first(grad_q, length), "seq", split_axis=0, concat_axis=1, tiled=True
    )
    d_queries = query_back.reshape(1, token_row_block, QUERY_HEADS * HEAD_SIZE)
    key_gradient = key_gradient_sum.reshape(1, token_row_block, KEY_VALUE_HEADS * HEAD_SIZE).astype(
        jnp.bfloat16
    )
    value_gradient = value_gradient_sum.reshape(
        1, token_row_block, KEY_VALUE_HEADS * HEAD_SIZE
    ).astype(jnp.bfloat16)
    exp_count = lax.axis_size("exp")
    ids_flat = expert_ids[0].reshape(-1)
    weight_flat = route_weight[0].reshape(-1)
    named_mask = (ids_flat[None, :] == jnp.arange(exp_count)[:, None]).astype(jnp.int32)
    slot_rank = jnp.cumsum(named_mask, axis=1, dtype=jnp.int32) - 1
    chosen = (
        (named_mask[:, None, :] == 1) & (slot_rank[:, None, :] == jnp.arange(CAP)[None, :, None])
    ).astype(jnp.float32)
    select = chosen.reshape(exp_count, CAP, token_row_block, TOPK).sum(-1).astype(jnp.bfloat16)
    mixing = (
        (chosen * weight_flat[None, None, :]).reshape(exp_count, CAP, token_row_block, TOPK).sum(-1)
    )
    send_tokens = jnp.einsum(
        "wct,td->wcd", select, normed[0], preferred_element_type=jnp.float32
    ).astype(jnp.bfloat16)
    send_grads = jnp.einsum(
        "wct,td->wcd", select, d_moe[0], preferred_element_type=jnp.float32
    ).astype(jnp.bfloat16)
    recv_tokens, recv_grads = (
        lax.all_to_all(send_tokens, "exp", split_axis=0, concat_axis=0, tiled=True),
        lax.all_to_all(send_grads, "exp", split_axis=0, concat_axis=0, tiled=True),
    )
    slot_rows = exp_count * CAP
    token_rows = recv_tokens.reshape(slot_rows, D)
    grad_rows_moe = recv_grads.reshape(slot_rows, D)
    gate_local = gate_w[0]
    up_local = up_w[0]
    down_local = down_t[0]
    gate_full, up_full, down_full = (
        lax.all_gather(gate_local, "seq", axis=0, tiled=True),
        lax.all_gather(up_local, "seq", axis=0, tiled=True),
        lax.all_gather(down_local, "seq", axis=0, tiled=True),
    )
    gate_val = jnp.dot(token_rows, gate_full, preferred_element_type=jnp.float32)
    up_val = jnp.dot(token_rows, up_full, preferred_element_type=jnp.float32)
    hidden_grad = jnp.dot(grad_rows_moe, down_full, preferred_element_type=jnp.float32)
    gate_grad, up_grad = activation_grads(gate_val, up_val, hidden_grad)
    slot_grad = back_columns(gate_grad, up_grad, gate_full, up_full)
    returned = lax.all_to_all(
        slot_grad.astype(jnp.bfloat16).reshape(exp_count, CAP, D),
        "exp",
        split_axis=0,
        concat_axis=0,
        tiled=True,
    )
    d_normed = jnp.einsum(
        "wct,wcd->td", mixing, returned.astype(jnp.float32), precision=lax.Precision.HIGHEST
    ).astype(jnp.bfloat16)[None]
    return (d_queries, key_gradient, value_gradient, d_normed)


def solution(mesh):
    in_specs = (
        P("exp", "seq", None),
        P("exp", "seq", None),
        P("exp", "seq", None),
        P("exp", "seq", None),
        P("exp", "seq", None),
        P("exp", "seq", None),
        P("exp", "seq", None),
        P("exp", "seq", None),
        P("exp", "seq", None),
        P("exp", "seq", None),
        P("exp", "seq", None),
        P("exp", "seq", None),
    )
    out_specs = (
        P("exp", "seq", None),
        P("exp", "seq", None),
        P("exp", "seq", None),
        P("exp", "seq", None),
    )
    return jax.shard_map(local, mesh=mesh, in_specs=in_specs, out_specs=out_specs, check_vma=False)
```

profile of v0, /device:TPU:1, one launch (start us, length us, event | category | flops | bytes accessed | tf_op | source)
XLA Modules:
  0.0 466.0 jit_solution(14096502495841969376)
XLA Ops:
  10.8 10.0 %all-to-all-start.3 = ((bf16[128,16,256]{0,2,1:T(8,128)(2,1)}), bf16[128,16,256]{0,2,1:T(8,128)(2,1)S(1)}, u32[]{:S(2)}, u32[]{:S(2)}) async-start(bf16[128,16,256]{0,2,1:T(8,128)(2,1)} %bitcast.14), calls=%async_computation.3 | async-start | bytes 2097152 | tf_op jit(solution)/shard_map/all_to_all | solution.py:144
  21.8 35.9 %all-to-all-done.3 = bf16[128,16,256]{0,2,1:T(8,128)(2,1)S(1)} async-done(((bf16[128,16,256]{0,2,1:T(8,128)(2,1)}), bf16[128,16,256]{0,2,1:T(8,128)(2,1)S(1)}, u32[]{:S(2)}, u32[]{:S(2)}) %all-to-all-start.3) | async-done | bytes 1048608 | tf_op jit(solution)/shard_map/all_to_all | solution.py:144
  58.9 4.9 %all-to-all-start.1 = ((bf16[128,16,256]{0,2,1:T(8,128)(2,1)}), bf16[128,16,256]{0,2,1:T(8,128)(2,1)S(1)}, u32[]{:S(2)}, u32[]{:S(2)}) async-start(bf16[128,16,256]{0,2,1:T(8,128)(2,1)} %bitcast.178), calls=%async_computation.1 | async-start | bytes 2097152 | tf_op jit(solution)/shard_map/all_to_all | solution.py:143
  66.1 34.3 %all-to-all-done.1 = bf16[128,16,256]{0,2,1:T(8,128)(2,1)S(1)} async-done(((bf16[128,16,256]{0,2,1:T(8,128)(2,1)}), bf16[128,16,256]{0,2,1:T(8,128)(2,1)S(1)}, u32[]{:S(2)}, u32[]{:S(2)}) %all-to-all-start.1) | async-done | bytes 1048608 | tf_op jit(solution)/shard_map/all_to_all | solution.py:143
  100.4 4.2 all-to-all-start
  106.9 30.9 %all-to-all-done = bf16[128,16,256]{0,2,1:T(8,128)(2,1)} async-done(((bf16[128,16,256]{0,2,1:T(8,128)(2,1)}), bf16[128,16,256]{0,2,1:T(8,128)(2,1)}, u32[]{:S(2)}, u32[]{:S(2)}) %all-to-all-start) | async-done | bytes 1048608 | tf_op jit(solution)/shard_map/all_to_all | solution.py:109
  137.8 6.4 %all-to-all-start.4 = ((bf16[128,16,256]{0,2,1:T(8,128)(2,1)}), bf16[128,16,256]{0,2,1:T(8,128)(2,1)S(1)}, u32[]{:S(2)}, u32[]{:S(2)}) async-start(bf16[128,16,256]{0,2,1:T(8,128)(2,1)} %bitcast.176), calls=%async_computation.4 | async-start | bytes 2097152 | tf_op jit(solution)/shard_map/all_to_all | solution.py:116
  145.2 4.5 reduce-window.6
  155.4 26.4 %all-to-all-done.4 = bf16[128,16,256]{0,2,1:T(8,128)(2,1)S(1)} async-done(((bf16[128,16,256]{0,2,1:T(8,128)(2,1)}), bf16[128,16,256]{0,2,1:T(8,128)(2,1)S(1)}, u32[]{:S(2)}, u32[]{:S(2)}) %all-to-all-start.4) | async-done | bytes 1048608 | tf_op jit(solution)/shard_map/all_to_all | solution.py:116
  181.9 5.9 %all-to-all-start.2 = ((bf16[128,16,256]{0,2,1:T(8,128)(2,1)}), bf16[128,16,256]{0,2,1:T(8,128)(2,1)}, u32[]{:S(2)}, u32[]{:S(2)}) async-start(bf16[128,16,256]{0,2,1:T(8,128)(2,1)} %bitcast.175), calls=%async_computation.2 | async-start | bytes 2097152 | tf_op jit(solution)/shard_map/all_to_all | solution.py:123
  216.5 4.5 all-to-all-done.2
  221.0 7.5 %all-to-all-start.9 = ((bf16[16,10,2048]{2,1,0:T(8,128)(2,1)}), bf16[16,10,2048]{2,1,0:T(8,128)(2,1)}, u32[]{:S(2)}, u32[]{:S(2)}) async-start(bf16[16,10,2048]{2,1,0:T(8,128)(2,1)} %copy.317), calls=%async_computation.9 | async-start | bytes 2097152 | tf_op jit(solution)/shard_map/all_to_all | solution.py:200
  261.9 6.8 %all-to-all-start.8 = ((bf16[16,10,2048]{2,1,0:T(8,128)(2,1)}), bf16[16,10,2048]{2,1,0:T(8,128)(2,1)}, u32[]{:S(2)}, u32[]{:S(2)}) async-start(bf16[16,10,2048]{2,1,0:T(8,128)(2,1)} %copy.316), calls=%async_computation.8 | async-start | bytes 2097152 | tf_op jit(solution)/shard_map/all_to_all | solution.py:201
  277.4 3.3 reduce.16
  285.2 3.3 all-to-all-done.8
  288.5 6.7 %all-to-all-start.5 = ((bf16[16,2,16384]{2,1,0:T(2,128)(2,1)}), bf16[16,2,16384]{2,1,0:T(2,128)(2,1)}, u32[]{:S(2)}, u32[]{:S(2)}) async-start(bf16[16,2,16384]{2,1,0:T(2,128)(2,1)} %reshape.469), calls=%async_computation.5 | async-start | bytes 2097152 | tf_op jit(solution)/shard_map/all_to_all | solution.py:171
  297.1 3.8 fusion.67
  302.4 7.3 %fusion.31 = f32[2,2048,128]{1,2,0:T(8,128)} fusion(f32[2,2048,128]{1,2,0:T(8,128)S(1)} %fusion.25, f32[2,512,2048]{2,1,0:T(8,128)} %copy-done.7, f32[2,512]{1,0:T(2,128)S(1)} %get-tuple-element.150, pred[512,2048]{1,0:T(8,128)(4,1)S(1)} %copy-done.19, bf16[2,2048,128]{2,1,0:T(8,128)(2,1)S(1)} %bitcast.154), kind=kOutput, calls=%fused_computation.41 | convolution fusion | flops 545783808 | bytes 13897728 | tf_op jit(solution)/shard_map/hqk,hqd->hkd/dot_general | solution.py:54
  309.8 6.2 %copy.309 = f32[2048,1,256]{2,1,0:T(1,128)} copy(f32[2048,1,256]{0,2,1:T(8,128)} %bitcast.180) | data formatting | bytes 4194304 | tf_op jit(solution)/shard_map/reshape | solution.py:85
  316.0 7.1 %all-to-all-done.5 = bf16[16,2,16384]{2,1,0:T(2,128)(2,1)} async-done(((bf16[16,2,16384]{2,1,0:T(2,128)(2,1)}), bf16[16,2,16384]{2,1,0:T(2,128)(2,1)}, u32[]{:S(2)}, u32[]{:S(2)}) %all-to-all-start.5) | async-done | bytes 1048608 | tf_op jit(solution)/shard_map/all_to_all | solution.py:171
  323.1 4.3 all-to-all-start.7
  333.4 3.2 fusion.29
  338.4 3.6 copy.302
  342.1 33.6 %all-to-all-done.7 = f32[2048,1,256]{2,1,0:T(1,128)} async-done(((f32[2048,1,256]{2,1,0:T(1,128)}), f32[2048,1,256]{2,1,0:T(1,128)}, u32[]{:S(2)}, u32[]{:S(2)}) %all-to-all-start.7) | async-done | bytes 2097184 | tf_op jit(solution)/shard_map/all_to_all | solution.py:157
  375.7 5.2 %all-to-all-start.6 = ((f32[2048,1,256]{2,1,0:T(1,128)}), f32[2048,1,256]{2,1,0:T(1,128)S(1)}, u32[]{:S(2)}, u32[]{:S(2)}) async-start(f32[2048,1,256]{2,1,0:T(1,128)} %copy.302), calls=%async_computation.6 | async-start | bytes 4194304 | tf_op jit(solution)/shard_map/all_to_all | solution.py:154
  384.5 5.1 %fusion.9 = f32[160,1536]{1,0:T(8,128)} fusion(bf16[160,2048]{1,0:T(8,128)(2,1)} %reshape.458, bf16[1,2048,1536]{2,1,0:T(8,128)(2,1)} %all-gather.7.cloned.1.call-done), kind=kOutput, calls=%fused_computation.13 | convolution fusion | flops 1006632960 | bytes 7929856 | tf_op jit(solution)/shard_map/dot_general | solution.py:216
  389.6 4.9 %fusion.3 = f32[160,1536]{1,0:T(8,128)} fusion(bf16[160,2048]{1,0:T(8,128)(2,1)S(1)} %reshape.459, bf16[1,2048,1536]{2,1,0:T(8,128)(2,1)} %all-gather.11.cloned.1.call-done), kind=kOutput, calls=%fused_computation.7 | convolution fusion | flops 1006632960 | bytes 7929856 | tf_op jit(solution)/shard_map/dot_general | solution.py:214
  394.5 9.5 %fusion.1 = f32[160,2048]{1,0:T(8,128)} fusion(bf16[1,2048,1536]{2,1,0:T(8,128)(2,1)} %all-gather.11.cloned.1.call-done, f32[160,1536]{1,0:T(8,128)} %fusion.9, bf16[160,2048]{1,0:T(8,128)(2,1)S(1)} %reshape.459, bf16[1,2048,1536]{2,1,0:T(8,128)(2,1)} %all-gather.9.cloned.1.call-done, f32[160,1536]{1,0:T(8,128)} %fusion.3), kind=kOutput, calls=%fused_computation.5 | convolution fusion | flops 2015723520 | bytes 16515072 | tf_op jit(solution)/shard_map/dot_general | solution.py:75
  404.0 5.9 %fusion.46 = bf16[160,2048]{1,0:T(8,128)(2,1)S(1)} fusion(f32[160,2048]{1,0:T(8,128)} %fusion.1, bf16[1,2048,1536]{2,1,0:T(8,128)(2,1)} %all-gather.9.cloned.1.call-done, f32[160,1536]{1,0:T(8,128)} %fusion.9, f32[160,1536]{1,0:T(8,128)} %fusion.3), kind=kOutput, calls=%fused_computation.47 | convolution fusion | flops 1008762880 | bytes 10223616 | tf_op jit(solution)/shard_map/dot_general | solution.py:77
  411.2 18.6 %all-to-all-done.6 = f32[2048,1,256]{2,1,0:T(1,128)S(1)} async-done(((f32[2048,1,256]{2,1,0:T(1,128)}), f32[2048,1,256]{2,1,0:T(1,128)S(1)}, u32[]{:S(2)}, u32[]{:S(2)}) %all-to-all-start.6) | async-done | bytes 2097184 | tf_op jit(solution)/shard_map/all_to_all | solution.py:154
  431.1 4.3 all-to-all-start.10
  435.4 4.3 reshape.470
  (160 shorter events, 128.7 us)
Async XLA Ops:
  7.2 147.9 %copy-start = (bf16[1,128,2048]{2,1,0:T(8,128)(2,1)S(1)}, bf16[1,128,2048]{2,1,0:T(8,128)(2,1)}, u32[]{:S(2)}) copy-start(bf16[1,128,2048]{2,1,0:T(8,128)(2,1)} %param.37) | copy-start | bytes 1572868
  7.2 377.3 %all-gather.7.cloned.1.call-start = ((), (), s32[]{:S(2)}) async-start(), calls=%async_computation.11 | async-start | bytes 6684672 | tf_op jit(solution)/shard_map/all_gather | solution.py:212
  7.9 381.7 %all-gather.11.cloned.1.call-start = ((), (), s32[]{:S(2)}) async-start(), calls=%async_computation.13 | async-start | bytes 6684672 | tf_op jit(solution)/shard_map/all_gather | solution.py:210
  10.8 46.9 %all-to-all-start.3 = ((bf16[128,16,256]{0,2,1:T(8,128)(2,1)}), bf16[128,16,256]{0,2,1:T(8,128)(2,1)S(1)}, u32[]{:S(2)}, u32[]{:S(2)}) async-start(bf16[128,16,256]{0,2,1:T(8,128)(2,1)} %bitcast.14), calls=%async_computation.3 | async-start | bytes 2097152 | tf_op jit(solution)/shard_map/all_to_all | solution.py:144
  58.9 41.5 %all-to-all-start.1 = ((bf16[128,16,256]{0,2,1:T(8,128)(2,1)}), bf16[128,16,256]{0,2,1:T(8,128)(2,1)S(1)}, u32[]{:S(2)}, u32[]{:S(2)}) async-start(bf16[128,16,256]{0,2,1:T(8,128)(2,1)} %bitcast.178), calls=%async_computation.1 | async-start | bytes 2097152 | tf_op jit(solution)/shard_map/all_to_all | solution.py:143
  63.8 81.1 %copy-start.22 = (s32[1,128,8]{1,2,0:T(8,128)S(1)}, s32[1,128,8]{1,2,0:T(8,128)}, u32[]{:S(2)}) copy-start(s32[1,128,8]{1,2,0:T(8,128)} %param.39) | copy-start | bytes 12292
  100.4 37.4 %copy-start.17 = (bf16[128,16,256]{0,2,1:T(8,128)(2,1)}, bf16[128,16,256]{0,2,1:T(8,128)(2,1)S(1)}, u32[]{:S(2)}) copy-start(bf16[128,16,256]{0,2,1:T(8,128)(2,1)S(1)} %all-to-all-done.1) | copy-start | bytes 3145732
  100.4 37.4 %all-to-all-start = ((bf16[128,16,256]{0,2,1:T(8,128)(2,1)}), bf16[128,16,256]{0,2,1:T(8,128)(2,1)}, u32[]{:S(2)}, u32[]{:S(2)}) async-start(bf16[128,16,256]{0,2,1:T(8,128)(2,1)} %bitcast.177), calls=%async_computation | async-start | bytes 2097152 | tf_op jit(solution)/shard_map/all_to_all | solution.py:109
  106.9 47.7 %copy-start.23 = (f32[1,128,8]{1,2,0:T(8,128)S(1)}, f32[1,128,8]{1,2,0:T(8,128)}, u32[]{:S(2)}) copy-start(f32[1,128,8]{1,2,0:T(8,128)} %param.40) | copy-start | bytes 12292
  137.8 44.0 %all-to-all-start.4 = ((bf16[128,16,256]{0,2,1:T(8,128)(2,1)}), bf16[128,16,256]{0,2,1:T(8,128)(2,1)S(1)}, u32[]{:S(2)}, u32[]{:S(2)}) async-start(bf16[128,16,256]{0,2,1:T(8,128)(2,1)} %bitcast.176), calls=%async_computation.4 | async-start | bytes 2097152 | tf_op jit(solution)/shard_map/all_to_all | solution.py:116
  144.2 250.3 %all-gather.9.cloned.1.call-start = ((), (), s32[]{:S(2)}) async-start(), calls=%async_computation.12 | async-start | bytes 6684672 | tf_op jit(solution)/shard_map/all_gather | solution.py:211
  181.9 39.1 %all-to-all-start.2 = ((bf16[128,16,256]{0,2,1:T(8,128)(2,1)}), bf16[128,16,256]{0,2,1:T(8,128)(2,1)}, u32[]{:S(2)}, u32[]{:S(2)}) async-start(bf16[128,16,256]{0,2,1:T(8,128)(2,1)} %bitcast.175), calls=%async_computation.2 | async-start | bytes 2097152 | tf_op jit(solution)/shard_map/all_to_all | solution.py:123
  221.0 40.9 %all-to-all-start.9 = ((bf16[16,10,2048]{2,1,0:T(8,128)(2,1)}), bf16[16,10,2048]{2,1,0:T(8,128)(2,1)}, u32[]{:S(2)}, u32[]{:S(2)}) async-start(bf16[16,10,2048]{2,1,0:T(8,128)(2,1)} %copy.317), calls=%async_computation.9 | async-start | bytes 2097152 | tf_op jit(solution)/shard_map/all_to_all | solution.py:200
  234.4 3.3 copy-start.12
  236.4 10.1 %copy-start.14 = (f32[2,512,1024]{2,1,0:T(8,128)}, f32[2,512,1024]{2,1,0:T(8,128)S(1)}, u32[]{:S(2)}) copy-start(f32[2,512,1024]{2,1,0:T(8,128)S(1)} %get-tuple-element.147) | copy-start | bytes 12582916
  239.2 20.1 %copy-start.2 = (f32[2,512,1536]{2,1,0:T(8,128)}, f32[2,512,1536]{2,1,0:T(8,128)S(1)}, u32[]{:S(2)}) copy-start(f32[2,512,1536]{2,1,0:T(8,128)S(1)} %get-tuple-element.145) | copy-start | bytes 18874372
  239.2 4.2 copy-start.10
  243.4 8.3 %copy-start.7 = (f32[2,512,2048]{2,1,0:T(8,128)}, f32[2,512,2048]{2,1,0:T(8,128)S(1)}, u32[]{:S(2)}) copy-start(f32[2,512,2048]{2,1,0:T(8,128)S(1)} %get-tuple-element.143) | copy-start | bytes 25165828
  248.3 3.4 copy-start.20
  261.9 26.6 %all-to-all-start.8 = ((bf16[16,10,2048]{2,1,0:T(8,128)(2,1)}), bf16[16,10,2048]{2,1,0:T(8,128)(2,1)}, u32[]{:S(2)}, u32[]{:S(2)}) async-start(bf16[16,10,2048]{2,1,0:T(8,128)(2,1)} %copy.316), calls=%async_computation.8 | async-start | bytes 2097152 | tf_op jit(solution)/shard_map/all_to_all | solution.py:201
  288.5 34.6 %all-to-all-start.5 = ((bf16[16,2,16384]{2,1,0:T(2,128)(2,1)}), bf16[16,2,16384]{2,1,0:T(2,128)(2,1)}, u32[]{:S(2)}, u32[]{:S(2)}) async-start(bf16[16,2,16384]{2,1,0:T(2,128)(2,1)} %reshape.469), calls=%async_computation.5 | async-start | bytes 2097152 | tf_op jit(solution)/shard_map/all_to_all | solution.py:171
  295.2 5.6 %slice-start = ((s8[6291456]{0:T(1024)(128)(4,1)}), s8[4194304]{0:T(1024)(128)(4,1)S(1)}, s32[]{:S(2)}) async-start(s8[6291456]{0:T(1024)(128)(4,1)} %bitcast.145), calls=%async_computation.14 | async-start | bytes 8388608
  297.1 3.8 slice-start.1
  297.1 3.8 copy-start.5
  309.8 17.6 %copy-start.6 = (bf16[2,512,512]{1,2,0:T(8,128)(2,1)S(1)}, bf16[2,512,512]{1,2,0:T(8,128)(2,1)}, u32[]{:S(2)}) copy-start(bf16[2,512,512]{1,2,0:T(8,128)(2,1)} %multiply_convert_fusion.3) | copy-start | bytes 3145732
  309.8 17.6 %copy-start.13 = (bf16[2048,2,128]{2,0,1:T(8,128)(2,1)S(1)}, bf16[2048,2,128]{2,0,1:T(8,128)(2,1)}, u32[]{:S(2)}) copy-start(bf16[2048,2,128]{2,0,1:T(8,128)(2,1)} %copy.274) | copy-start | bytes 3145732
  323.1 52.6 %all-to-all-start.7 = ((f32[2048,1,256]{2,1,0:T(1,128)}), f32[2048,1,256]{2,1,0:T(1,128)}, u32[]{:S(2)}, u32[]{:S(2)}) async-start(f32[2048,1,256]{2,1,0:T(1,128)} %copy.309), calls=%async_computation.7 | async-start | bytes 4194304 | tf_op jit(solution)/shard_map/all_to_all | solution.py:157
  327.4 3.7 copy-start.3
  375.7 54.1 %all-to-all-start.6 = ((f32[2048,1,256]{2,1,0:T(1,128)}), f32[2048,1,256]{2,1,0:T(1,128)S(1)}, u32[]{:S(2)}, u32[]{:S(2)}) async-start(f32[2048,1,256]{2,1,0:T(1,128)} %copy.302), calls=%async_computation.6 | async-start | bytes 4194304 | tf_op jit(solution)/shard_map/all_to_all | solution.py:154
  431.1 25.5 %all-to-all-start.10 = ((bf16[16,10,2048]{2,1,0:T(8,128)(2,1)}), bf16[16,10,2048]{2,1,0:T(8,128)(2,1)}, u32[]{:S(2)}, u32[]{:S(2)}) async-start(bf16[16,10,2048]{2,1,0:T(8,128)(2,1)} %reshape.460), calls=%async_computation.10 | async-start | bytes 2097152 | tf_op jit(solution)/shard_map/all_to_all | solution.py:219
  446.9 5.5 %copy-start.9 = (f32[2048,1,256]{2,1,0:T(1,128)S(1)}, f32[2048,1,256]{2,1,0:T(1,128)}, u32[]{:S(2)}) copy-start(f32[2048,1,256]{2,1,0:T(1,128)} %copy-done.8) | copy-start | bytes 6291460
  452.4 6.9 %copy-start.1 = (bf16[1,128,2048]{2,1,0:T(8,128)(2,1)S(1)}, bf16[1,128,2048]{2,1,0:T(8,128)(2,1)}, u32[]{:S(2)}) copy-start(bf16[1,128,2048]{2,1,0:T(8,128)(2,1)} %param.37) | copy-start | bytes 1572868
  (8 other events, 15.3 us)
Sparse Core Ops, SparseCore 0:
  9.8 90.2 all-gather.6
  101.9 82.6 all-gather.10
  186.5 58.8 all-gather.8
where the time goes:
time: 472 us; the launch traced here: 466 us
  waiting for transfers between devices  197 us (42%)
  local copies, waits for them, and re-layouts  90.3 us (19%)
  matrix products  76.8 us (16%)
  starting transfers between devices  66.5 us (14%)
  other arithmetic  21.2 us (4%)
  between operations  14.6 us (3%)
    all_to_all x1, waiting for transfers between devices, local(): lax.all_to_all(value_send, 'seq', split_axis=1, concat_axis=0, tiled=True)  35.9 us
    all_to_all x1, waiting for transfers between devices, local(): lax.all_to_all(key_send, 'seq', split_axis=1, concat_axis=0, tiled=True)  34.3 us
    all_to_all x1, waiting for transfers between devices, local(): lax.all_to_all(tokens_first(value_gradient_part, length), 'seq', split_ax...  33.6 us
    all_to_all x1, waiting for transfers between devices, local(): lax.all_to_all(queries[0].reshape(token_row_block, seq_count, slot_width)...  30.9 us
    unnamed x65, local copies, waits for them, and re-layouts  30.4 us
    all_to_all x1, waiting for transfers between devices, local(): lax.all_to_all(attn_out[0].reshape(token_row_block, seq_count, slot_width...  26.4 us
    all_to_all x1, waiting for transfers between devices, local(): lax.all_to_all(tokens_first(key_gradient_part, length), 'seq', split_axis...  18.6 us
    dot_general x4, matrix products, head_gradients(): jnp.einsum('hqk,hqd->hkd', weights_low, grad_block, preferred_element_typ...  14.2 us
  transfers between devices with their start and end apart: 14, of which 9 were waited for; matrix products, arithmetic and copies ran while one was open for 38% of the time, Pallas kernels for 0%

commit v1 on v0

v1 whole, which is shorter than its diff:
```python
import functools
import math

import jax
import jax.numpy as jnp
from jax import lax
from jax.experimental import pallas as pl
from jax.experimental.pallas import tpu as pltpu
from jax.sharding import PartitionSpec as P

MESH = pl.DeviceIdType.MESH
F32 = jnp.float32
BF16 = jnp.bfloat16
HEAD = 128
TOK = 128
PAIR = 2 * TOK
SLOT = 16
LOW = -1e30
MINOR = (((1,), (1,)), ((), ()))
MAJOR = (((0,), (0,)), ((), ()))


def dot(a, b, dims=(((1,), (0,)), ((), ()))):
    return lax.dot_general(a, b, dims, preferred_element_type=F32)


def kernel(
    nz, ne,
    q_in, k_in, v_in, o_in, do_in, x_in, g_in, ids, route, gate_in, up_in, down_in,
    dq_out, dk_out, dv_out, dn_out,
    W, KV, KT, Q, DO, OF, DOF, RDX, RD, PB, MJ, DKV, DQT, DQ, SB, RB, FB, XG, XS, XR, ACC, GU, RS, RR, MIX, OUT,
    loc, sib_s, sib_r, wgt_s, wgt_r, wsb_s, wsb_r, kv_s, kv_r, gr_s, gr_r, tok_s, tok_r, ret_s, ret_r,
):
    half = nz // 2
    nk = 3 * half
    groups = Q.shape[1] // HEAD
    width = groups * HEAD
    hid = W.shape[3]
    model = W.shape[1] * W.shape[2]
    scale = 1.0 / math.sqrt(HEAD)
    log2e = math.log2(math.e)

    s = lax.axis_index("seq")
    e = lax.axis_index("exp")
    z = lax.div(s, 2)
    c = lax.rem(s, 2)
    other = 1 - c

    def plane(delta):
        return lax.rem(z + delta + nz, nz)

    near = (
        {"seq": 2 * plane(1) + c},
        {"seq": 2 * plane(-1) + c},
    )
    sibling = {"seq": 2 * z + other}

    def peer(p):
        return lax.rem(e + p, ne)

    def send(src, dst, ss, rs, to):
        return pltpu.make_async_remote_copy(
            src_ref=src, dst_ref=dst, send_sem=ss, recv_sem=rs, device_id=to, device_id_type=MESH
        )

    def arrived(dst, rs):
        send(dst, dst, rs, rs, sibling).wait_recv()

    def sent(src, ss):
        send(src, src, ss, ss, sibling).wait_send()

    mine = pl.ds(pl.multiple_of(c * TOK, TOK), TOK)
    theirs = pl.ds(pl.multiple_of(other * TOK, TOK), TOK)
    my_heads = pl.ds(pl.multiple_of(c * width, width), width)
    their_heads = pl.ds(pl.multiple_of(other * width, width), width)
    my_head = pl.ds(pl.multiple_of(c * HEAD, HEAD), HEAD)
    their_head = pl.ds(pl.multiple_of(other * HEAD, HEAD), HEAD)

    local = [
        (k_in.at[0, :, my_head], KV.at[z, 0, mine]),
        (v_in.at[0, :, my_head], KV.at[z, 1, mine]),
        (x_in.at[0], XG.at[0]),
        (g_in.at[0], XG.at[1]),
        (o_in.at[0], OF),
        (do_in.at[0], DOF),
        (q_in.at[0, :, my_heads], Q.at[mine]),
        (do_in.at[0, :, my_heads], DO.at[mine]),
        (gate_in.at[0], W.at[0, s]),
        (up_in.at[0], W.at[1, s]),
        (down_in.at[0], W.at[2, s]),
    ]
    local = [pltpu.make_async_copy(a, b, loc.at[i]) for i, (a, b) in enumerate(local)]
    for copy in local:
        copy.start()

    barrier = pltpu.get_barrier_semaphore()
    for to in (*near, sibling):
        pl.semaphore_signal(barrier, inc=1, device_id=to, device_id_type=MESH)

    def greet(p, carry):
        pl.semaphore_signal(barrier, inc=1, device_id={"exp": peer(p)}, device_id_type=MESH)
        return carry

    lax.fori_loop(1, ne, greet, 0)
    pl.semaphore_wait(barrier, 3 + ne - 1)

    swap = [
        send(k_in.at[0, :, their_head], KV.at[z, 0, mine], sib_s.at[0], sib_r.at[0], sibling),
        send(v_in.at[0, :, their_head], KV.at[z, 1, mine], sib_s.at[1], sib_r.at[1], sibling),
        send(q_in.at[0, :, their_heads], Q.at[mine], sib_s.at[2], sib_r.at[2], sibling),
        send(do_in.at[0, :, their_heads], DO.at[mine], sib_s.at[3], sib_r.at[3], sibling),
    ]
    for copy in swap:
        copy.start()

    def kv_region(d, hop):
        at = plane(-hop if d == 0 else hop)
        return KV.at[at] if hop < half else KV.at[at, d]

    def kv_forward(d, hop):
        at = plane(-hop if d == 0 else hop)
        region = KV.at[at] if hop + 1 < half else KV.at[at, d]
        send(region, region, kv_s.at[d, hop], kv_r.at[d, hop], near[d]).start()

    def kv_sent(d, hop):
        at = plane(-hop if d == 0 else hop)
        region = KV.at[at] if hop + 1 < half else KV.at[at, d]
        sent(region, kv_s.at[d, hop])

    def kv_step(hop):
        for d in range(2):
            arrived(kv_region(d, hop), kv_r.at[d, hop - 1])
            if hop < half:
                kv_forward(d, hop)

    own = (gate_in, up_in, down_in)

    def w_own(d, m):
        return send(own[m].at[0], W.at[m, s], wgt_s.at[d, m], wgt_r.at[d, m], near[d])

    def w_own_sibling(m):
        return send(own[m].at[0], W.at[m, s], wsb_s.at[0, nk + m], wsb_r.at[0, nk + m], sibling)

    def w_region(d, k, core, rows_of=None):
        hop = lax.div(k, 3) + 1
        at = plane(-hop if d == 0 else hop)
        region = W.at[lax.rem(k, 3), 2 * at + core]
        if rows_of is None:
            return region
        rows = W.shape[2] // 2
        return region.at[pl.ds(rows * rows_of, rows)]

    def w_arrives(d, k, core):
        last = not isinstance(k, jax.Array) and k >= nk - 3
        return w_region(d, k, core, d if last else None)

    def w_leaves(d, k):
        last = not isinstance(k, jax.Array) and k + 3 >= nk - 3
        return w_region(d, k, c, d if last else None)

    def pump(k):
        for d in range(2):
            region = w_arrives(d, k, c)
            arrived(region, wgt_r.at[d, k])
            if isinstance(k, jax.Array) or k + 3 < nk:
                leaving = w_leaves(d, k)
                send(leaving, leaving, wgt_s.at[d, k + 3], wgt_r.at[d, k + 3], near[d]).start()
            send(region, region, wsb_s.at[d, k], wsb_r.at[d, k], sibling).start()

    def routing():
        lane = lax.broadcasted_iota(jnp.int32, (TOK, ne * SLOT), 1)
        expert = lax.shift_right_logical(lane, 4)
        slot = lax.bitwise_and(lane, SLOT - 1).astype(F32)
        named = jnp.zeros((TOK, ne * SLOT), F32)
        weight = jnp.zeros((TOK, ne * SLOT), F32)
        for rank in range(ids.shape[2]):
            hit = ids[0, :, rank : rank + 1] == expert
            named = jnp.where(hit, 1.0, named)
            weight = jnp.where(hit, route[0, :, rank : rank + 1], weight)
        row = lax.broadcasted_iota(jnp.int32, (TOK, TOK), 0)
        col = lax.broadcasted_iota(jnp.int32, (TOK, TOK), 1)
        earlier = (col < row).astype(F32).astype(BF16)
        place = dot(earlier, named.astype(BF16))
        select = jnp.where((named > 0.0) & (place == slot), 1.0, 0.0)
        mixing = select * weight
        high = mixing.astype(BF16)
        MIX[0] = high
        MIX[1] = (mixing - high.astype(F32)).astype(BF16)
        return select.astype(BF16)

    def token_copy(p):
        to = peer(p)
        return send(
            XS.at[:, pl.ds(pl.multiple_of(to * SLOT, SLOT), SLOT)],
            XR.at[:, pl.ds(pl.multiple_of(e * SLOT, SLOT), SLOT)],
            tok_s.at[p], tok_r.at[p], {"exp": to},
        )

    def token_arrived(p):
        src = lax.rem(e - p + ne, ne)
        arrived(XR.at[:, pl.ds(pl.multiple_of(src * SLOT, SLOT), SLOT)], tok_r.at[p])

    def loop(lo, hi, f):
        def body(i, carry):
            f(i)
            return carry

        lax.fori_loop(lo, hi, body, 0)

    local[0].wait()
    local[1].wait()
    arrived(KV.at[z, 0, theirs], sib_r.at[0])
    arrived(KV.at[z, 1, theirs], sib_r.at[1])
    for d in range(2):
        kv_forward(d, 0)
    for m in range(3):
        w_own_sibling(m).start()
    local[2].wait()
    local[3].wait()
    select = routing()
    for i in range(2):
        for n in range(model // 512):
            cols = pl.ds(512 * n, 512)
            XS[i, :, cols] = dot(select, XG[i, :, cols], MAJOR).astype(BF16)
    loop(1, ne, lambda p: token_copy(p).start())
    my_slots = pl.ds(pl.multiple_of(e * SLOT, SLOT), SLOT)
    XR[:, my_slots, :] = XS[:, my_slots, :]
    kv_step(1)
    for d in range(2):
        w_own(d, 0).start()

    local[4].wait()
    local[5].wait()
    ones = jnp.ones((8, HEAD), BF16)

    def head_dot(col):
        cols = pl.ds(pl.multiple_of(col, HEAD), HEAD)
        product = OF[:, cols].astype(F32) * DOF[:, cols].astype(F32)
        high = product.astype(BF16)
        low = (product - high.astype(F32)).astype(BF16)
        return dot(ones, high, MINOR) + dot(ones, low, MINOR)

    def both_dots(h):
        RDX[h] = head_dot((other * groups + h) * HEAD)
        RD[h, :, mine] = head_dot((c * groups + h) * HEAD)

    loop(0, groups, both_dots)
    swap_dot = send(RDX, RD.at[:, :, mine], sib_s.at[4], sib_r.at[4], sibling)
    swap_dot.start()
    kv_step(2)
    for d in range(2):
        w_own(d, 1).start()
    DKV[...] = jnp.zeros(DKV.shape, F32)
    for hop in range(3, half):
        kv_step(hop)
    for d in range(2):
        w_own(d, 2).start()
    if half > 2:
        kv_step(half)

    def turn(j):
        KT[j] = KV[j, 0].T

    loop(0, nz, turn)
    local[6].wait()
    local[7].wait()
    arrived(Q.at[theirs], sib_r.at[2])
    arrived(DO.at[theirs], sib_r.at[3])
    arrived(RD.at[:, :, theirs], sib_r.at[4])

    in_loop = max(0, nk - 6)

    def head(h):
        cols = pl.ds(pl.multiple_of(h * HEAD, HEAD), HEAD)
        queries = Q[:, cols]
        grads = DO[:, cols]
        dots = RD[h]

        def scores(j, carry, diagonal):
            top, total = carry
            value = dot(KV[j, 0], queries, MINOR) * (scale * log2e)
            if diagonal:
                key = lax.broadcasted_iota(jnp.int32, (PAIR, PAIR), 0)
                query = lax.broadcasted_iota(jnp.int32, (PAIR, PAIR), 1)
                value = jnp.where(key <= query, value, LOW)
            value = value.reshape(PAIR // 8, 8, PAIR)
            new = jnp.maximum(top, jnp.max(value, axis=0))
            value = jnp.exp2(value - new[None])
            total = total * jnp.exp2(top - new) + jnp.sum(value, axis=0)
            PB[j] = value.reshape(PAIR, PAIR)
            MJ[j] = new
            return new, total

        carry = (jnp.full((8, PAIR), LOW, F32), jnp.zeros((8, PAIR), F32))
        carry = lax.fori_loop(0, z, lambda j, x: scores(j, x, False), carry)
        top, total = scores(z, carry, True)
        peak = jnp.max(top, axis=0, keepdims=True)
        total = jnp.sum(total * jnp.exp2(top - peak), axis=0, keepdims=True)
        inverse = 1.0 / total
        DQT[...] = jnp.zeros(DQT.shape, F32)

        def gradients(j):
            factor = jnp.exp2(MJ[j] - peak) * inverse
            weights = PB[j].reshape(PAIR // 8, 8, PAIR) * factor[None]
            grad = dot(KV[j, 1], grads, MINOR).reshape(PAIR // 8, 8, PAIR)
            low = (weights * (grad - dots[None])).reshape(PAIR, PAIR).astype(BF16)
            DKV[j, 1] += dot(weights.reshape(PAIR, PAIR).astype(BF16), grads)
            DKV[j, 0] += dot(low, queries)
            DQT[...] += dot(KT[j], low)

        loop(0, z + 1, gradients)
        DQ[:, cols] = (DQT[...] * scale).T.astype(BF16)

        @pl.when((lax.rem(h, 2) == 1) & (lax.div(h, 2) < in_loop))
        def _():
            pump(lax.div(h, 2))

    loop(0, groups, head)

    dq_mine = pltpu.make_async_copy(DQ.at[mine], dq_out.at[0, :, my_heads], loc.at[11])
    dq_theirs = send(DQ.at[theirs], dq_out.at[0, :, my_heads], sib_s.at[5], sib_r.at[5], sibling)
    dq_mine.start()
    dq_theirs.start()

    def grad_step(r):
        for d in range(2):
            t = half - r
            at = plane(r if d == 0 else -r)
            if r == half:
                SB[d, t, d] = DKV[at, d].astype(BF16)
            elif r == half - 1:
                arrived(RB.at[d, t - 1, d], gr_r.at[d, t - 1])
                SB[d, t, d] = (DKV[at, d] + RB[d, t - 1, d].astype(F32)).astype(BF16)
                SB[d, t, 1 - d] = DKV[at, 1 - d].astype(BF16)
            else:
                arrived(RB.at[d, t - 1], gr_r.at[d, t - 1])
                SB[d, t] = (DKV[at] + RB[d, t - 1].astype(F32)).astype(BF16)
            grad_copy(d, t).start()

    def grad_copy(d, t):
        if t == 0:
            return send(SB.at[d, 0, d], RB.at[d, 0, d], gr_s.at[d, 0], gr_r.at[d, 0], near[d])
        return send(SB.at[d, t], RB.at[d, t], gr_s.at[d, t], gr_r.at[d, t], near[d])

    def grad_end():
        t = half - 1
        for d in range(2):
            arrived(RB.at[d, t], gr_r.at[d, t])
        total = DKV[z] + RB[0, t].astype(F32) + RB[1, t].astype(F32)
        FB[0] = (total[0] * scale).astype(BF16)
        FB[1] = total[1].astype(BF16)
        copies = []
        for i, out in enumerate((dk_out, dv_out)):
            copies.append(pltpu.make_async_copy(FB.at[i, mine], out.at[0, :, my_head], loc.at[12 + i]))
            copies.append(send(FB.at[i, theirs], out.at[0, :, my_head], sib_s.at[6 + i], sib_r.at[6 + i], sibling))
        for copy in copies:
            copy.start()
        return copies

    def gather_wait(d, k):
        arrived(w_arrives(d, k, other), wsb_r.at[d, k])

    def add(m, planes, first=False):
        for n in range(hid // 256):
            cols = pl.ds(256 * n, 256)
            total = None if first else ACC[m, :, cols]
            for at in planes:
                part = dot(
                    XR[m // 2, :, pl.ds(pl.multiple_of(at * PAIR, PAIR), PAIR)],
                    W[m, pl.ds(2 * at, 2), :, cols].reshape(PAIR, 256),
                )
                total = part if total is None else total + part
            ACC[m, :, cols] = total

    def add_hop(hop, m):
        k = 3 * (hop - 1) + m
        for d in range(2):
            gather_wait(d, k)
        add(m, [plane(-hop), plane(hop)] if hop < half else [plane(hop)])

    for k in range(in_loop, nk - 6):
        pump(k)
    grad_step(half)
    loop(1, ne, token_arrived)
    for m in range(3):
        local[8 + m].wait()
        arrived(W.at[m, 2 * z + other], wsb_r.at[0, nk + m])
        add(m, [z], first=True)
    rest = list(range(half - 1, 0, -1))
    done = 0
    hops = [(hop, m) for hop in range(1, half + 1) for m in range(3)]
    final = []
    for step in range(nk - 6, nk):
        if rest:
            grad_step(rest.pop(0))
            if not rest:
                final = None
        elif final is None:
            final = grad_end()
        while done < step:
            add_hop(*hops[done])
            done += 1
            if done % 3 == 0:
                break
        pump(step)
    if final is None:
        final = grad_end()
    while done < nk:
        add_hop(*hops[done])
        done += 1

    rows = 16

    def activate(i):
        at = pl.ds(pl.multiple_of(i * rows, rows), rows)
        gate, up, grad = ACC[0, at, :], ACC[1, at, :], ACC[2, at, :]
        sig = 1.0 / (1.0 + jnp.exp(-gate))
        GU[0, at, :] = (grad * up * sig * (1.0 + gate * (1.0 - sig))).astype(BF16)
        GU[1, at, :] = (grad * (gate * sig)).astype(BF16)

    loop(0, ne * SLOT // rows, activate)

    parts = ret_s.shape[0]
    span = model // parts

    def ret_copy(i, p):
        to = peer(p)
        cols = pl.ds(span * i, span)
        return send(
            RS.at[pl.ds(pl.multiple_of(to * SLOT, SLOT), SLOT), cols],
            RR.at[pl.ds(pl.multiple_of(e * SLOT, SLOT), SLOT), cols],
            ret_s.at[i, p], ret_r.at[i, p], {"exp": to},
        )

    def ret_arrived(i, p):
        src = lax.rem(e - p + ne, ne)
        arrived(RR.at[pl.ds(pl.multiple_of(src * SLOT, SLOT), SLOT), pl.ds(span * i, span)], ret_r.at[i, p])

    for i in range(parts):
        for n in range(i * span // PAIR, (i + 1) * span // PAIR):
            back = dot(GU[0], W[0, 2 * n : 2 * n + 2].reshape(PAIR, hid), MINOR) + dot(
                GU[1], W[1, 2 * n : 2 * n + 2].reshape(PAIR, hid), MINOR
            )
            RS[:, PAIR * n : PAIR * n + PAIR] = back.astype(BF16)
        loop(1, ne, lambda p: ret_copy(i, p).start())
        cols = pl.ds(span * i, span)
        RR[my_slots, cols] = RS[my_slots, cols]
    outs = []
    for i in range(parts):
        loop(1, ne, lambda p: ret_arrived(i, p))
        cols = pl.ds(span * i, span)
        back = RR[:, cols]
        OUT[:, cols] = (dot(MIX[0], back) + dot(MIX[1], back)).astype(BF16)
        copy = pltpu.make_async_copy(OUT.at[:, cols], dn_out.at[0, :, cols], loc.at[14 + i])
        copy.start()
        outs.append(copy)

    for copy in swap:
        copy.wait_send()
    swap_dot.wait_send()
    for d in range(2):
        for hop in range(half):
            kv_sent(d, hop)
        for m in range(3):
            w_own(d, m).wait_send()
        for k in range(nk - 3):
            sent(w_leaves(d, k), wgt_s.at[d, k + 3])
        for k in range(nk):
            sent(w_arrives(d, k, c), wsb_s.at[d, k])
        for t in range(half):
            grad_copy(d, t).wait_send()
    for m in range(3):
        w_own_sibling(m).wait_send()
    loop(1, ne, lambda p: token_copy(p).wait_send())
    for i in range(parts):
        loop(1, ne, lambda p: ret_copy(i, p).wait_send())
    dq_mine.wait()
    dq_theirs.wait_send()
    arrived(dq_out.at[0, :, their_heads], sib_r.at[5])
    for i, out in enumerate((dk_out, dv_out)):
        final[2 * i].wait()
        final[2 * i + 1].wait_send()
        arrived(out.at[0, :, their_head], sib_r.at[6 + i])
    for copy in outs:
        copy.wait()


def local(nz, ne, queries, keys, values, attn_out, d_attn, normed, d_moe, ids, route, gate_w, up_w, down_t):
    half = nz // 2
    nk = 3 * half
    heads = queries.shape[2]
    width = heads // 2
    groups = width // HEAD
    model = normed.shape[2]
    rows, hid = gate_w.shape[1:]
    slots = ne * SLOT
    parts = 4
    dma = pltpu.SemaphoreType.DMA
    anywhere = pl.BlockSpec(memory_space=pl.ANY)
    vmem = pl.BlockSpec(memory_space=pltpu.VMEM)
    scratch = [
        pltpu.VMEM((3, 2 * nz, rows, hid), BF16),
        pltpu.VMEM((nz, 2, PAIR, HEAD), BF16),
        pltpu.VMEM((nz, HEAD, PAIR), BF16),
        pltpu.VMEM((PAIR, width), BF16),
        pltpu.VMEM((PAIR, width), BF16),
        pltpu.VMEM((TOK, heads), BF16),
        pltpu.VMEM((TOK, heads), BF16),
        pltpu.VMEM((groups, 8, TOK), F32),
        pltpu.VMEM((groups, 8, PAIR), F32),
        pltpu.VMEM((nz, PAIR, PAIR), F32),
        pltpu.VMEM((nz, 8, PAIR), F32),
        pltpu.VMEM((nz, 2, PAIR, HEAD), F32),
        pltpu.VMEM((HEAD, PAIR), F32),
        pltpu.VMEM((PAIR, width), BF16),
        pltpu.VMEM((2, half, 2, PAIR, HEAD), BF16),
        pltpu.VMEM((2, half, 2, PAIR, HEAD), BF16),
        pltpu.VMEM((2, PAIR, HEAD), BF16),
        pltpu.VMEM((2, TOK, model), BF16),
        pltpu.VMEM((2, slots, model), BF16),
        pltpu.VMEM((2, slots, model), BF16),
        pltpu.VMEM((3, slots, hid), F32),
        pltpu.VMEM((2, slots, hid), BF16),
        pltpu.VMEM((slots, model), BF16),
        pltpu.VMEM((slots, model), BF16),
        pltpu.VMEM((2, TOK, slots), BF16),
        pltpu.VMEM((TOK, model), BF16),
        dma((14 + parts,)),
        dma((8,)), dma((8,)),
        dma((2, nk)), dma((2, nk)),
        dma((2, nk + 3)), dma((2, nk + 3)),
        dma((2, half)), dma((2, half)),
        dma((2, half)), dma((2, half)),
        dma((ne,)), dma((ne,)),
        dma((parts, ne)), dma((parts, ne)),
    ]
    return pl.pallas_call(
        functools.partial(kernel, nz, ne),
        out_shape=(
            jax.ShapeDtypeStruct(queries.shape, BF16),
            jax.ShapeDtypeStruct(keys.shape, BF16),
            jax.ShapeDtypeStruct(values.shape, BF16),
            jax.ShapeDtypeStruct(normed.shape, BF16),
        ),
        in_specs=[anywhere] * 7 + [vmem] * 2 + [anywhere] * 3,
        out_specs=[anywhere] * 4,
        scratch_shapes=scratch,
        compiler_params=pltpu.CompilerParams(
            collective_id=0, has_side_effects=True, vmem_limit_bytes=60 * 1024 * 1024
        ),
        name="layer_backward",
    )(queries, keys, values, attn_out, d_attn, normed, d_moe, ids, route, gate_w, up_w, down_t)


def solution(mesh):
    nz, ne = mesh.shape["seq"] // 2, mesh.shape["exp"]
    spec = P("exp", "seq", None)
    return jax.shard_map(
        functools.partial(local, nz, ne),
        mesh=mesh,
        in_specs=(spec,) * 12,
        out_specs=(spec,) * 4,
        check_vma=False,
    )
```

time: 472 us -> 185 us (0.39); the launches traced: 466 us -> 184 us
  waiting for transfers between devices: 197 us -> 0 us
  Pallas kernels: 0 us -> 177 us
  local copies, waits for them, and re-layouts: 90.3 us -> 6.79 us
  matrix products: 76.8 us -> 0 us
  starting transfers between devices: 66.5 us -> 0 us
  other arithmetic: 21.2 us -> 0 us
  between operations: 14.6 us -> 0.67 us
    all_to_all x11 -> x0, waiting for transfers between devices: 195 us -> none  [the longest x1 35.9 us: local(): lax.all_to_all(value_send, 'seq', split_axis=1, concat_axis=0, tiled=True)]
    pallas_call x0 -> x1, Pallas kernels: none -> 177 us  [local(): pl.pallas_call(functools.partial(kernel, nz, ne), out_shape=(jax.ShapeDty...]
    dot_general x27 -> x0, matrix products: 76.8 us -> none  [the longest x4 14.2 us: head_gradients(): jnp.einsum('hqk,hqd->hkd', weights_low, grad_block, preferred_element_typ...]
    all_to_all x11 -> x0, starting transfers between devices: 66.3 us -> none  [the longest x1 9.98 us: local(): lax.all_to_all(value_send, 'seq', split_axis=1, concat_axis=0, tiled=True)]
    reshape x14 -> x0, local copies, waits for them, and re-layouts: 26.9 us -> none  [the longest x8 11.7 us: heads_first(): arrived.reshape(length, head_count, HEAD_SIZE)]
    unnamed x65 -> x14, local copies, waits for them, and re-layouts: 30.4 us -> 6.79 us
    all_to_all x7 -> x0, local copies, waits for them, and re-layouts: 14 us -> none  [the longest x1 3.07 us: local(): lax.all_to_all(tokens_first(value_gradient_part, length), 'seq', split_ax...]
    convert_element_type x5 -> x0, local copies, waits for them, and re-layouts: 8.39 us -> none  [the longest x3 5.61 us: head_gradients(): output_heads.astype(jnp.float32)]
  transfers between devices with their start and end apart: 14 -> 0, of which waited for: 9 -> 0; matrix products, arithmetic and copies ran while one was open for 38% -> 0% of each run, Pallas kernels for 0% -> 0%
where the time goes in v1:
time: 185 us; the launch traced here: 184 us
  Pallas kernels  177 us (96%)
  local copies, waits for them, and re-layouts  6.79 us (4%)
    pallas_call x1, Pallas kernels, local(): pl.pallas_call(functools.partial(kernel, nz, ne), out_shape=(jax.ShapeDty...  177 us
    unnamed x14, local copies, waits for them, and re-layouts  6.79 us

profile of v1, /device:TPU:1, one launch (start us, length us, event | category | flops | bytes accessed | tf_op | source)
XLA Modules:
  0.0 184.4 jit_solution(2196186237326272324)
XLA Ops:
  0.6 0.0 copy-start.3
  0.6 1.4 copy.16.ids
  2.1 0.0 copy-done.3
  2.1 0.7 copy.17.route
  2.8 177.0 %layer_backward.1 = (bf16[1,128,4096]{2,1,0:T(8,128)(2,1)}, bf16[1,128,256]{2,1,0:T(8,128)(2,1)}, bf16[1,128,256]{2,1,0:T(8,128)(2,1)}, bf16[1,128,2048]{2,1,0:T(8,128)(2,1)}) custom-call(bf16[1,128,4096]{2,1,0:T(8,128)(2,1)} %q_in.1, bf16[1,128,256]{2,1,0:T(8,128)(2,1)} %k_in.1, bf16[1,128,256]{2,1,0:T(8,128)(2,1)} %v_in.1, bf16[1,128,4096]{2,1,0:T(8,128)(2,1)} %o_in.1, ...), custom_call_target="tpu_custom_call" | custom-call | tf_op jit(solution)/shard_map/layer_backward/pallas_call | solution.py:537
  179.8 0.0 copy-start.2
  179.8 0.0 copy-start
  179.8 2.3 %copy.22 = bf16[1,128,4096]{2,1,0:T(8,128)(2,1)} copy(bf16[1,128,4096]{2,1,0:T(8,128)(2,1)} %get-tuple-element.8) | data formatting | bytes 2097152
  182.2 0.0 copy-done.2
  182.2 0.0 copy-start.1
  182.2 0.6 copy.23
  182.8 0.2 copy-done.1
  183.0 0.6 copy.24
  183.6 0.0 copy-done
  183.7 0.8 copy.25
Async XLA Ops:
  0.6 1.4 copy-start.3
  179.8 2.4 %copy-start.2 = (bf16[1,128,256]{2,1,0:T(8,128)(2,1)S(1)}, bf16[1,128,256]{2,1,0:T(8,128)(2,1)}, u32[]{:S(2)}) copy-start(bf16[1,128,256]{2,1,0:T(8,128)(2,1)} %get-tuple-element.9) | copy-start | bytes 196612
  179.8 3.9 %copy-start = (bf16[1,128,2048]{2,1,0:T(8,128)(2,1)S(1)}, bf16[1,128,2048]{2,1,0:T(8,128)(2,1)}, u32[]{:S(2)}) copy-start(bf16[1,128,2048]{2,1,0:T(8,128)(2,1)} %get-tuple-element.11) | copy-start | bytes 1572868
  182.2 0.9 copy-start.1

commit v2 on v1

--- a/solution.py
+++ b/solution.py
@@ -15,7 +15,9 @@
 TOK = 128
 PAIR = 2 * TOK
 SLOT = 16
+CAP = 10
 LOW = -1e30
+PIECES = ((0, 0, 48), (0, 48, 48), (0, 96, 32), (1, 0, 48), (1, 48, 80), (2, 0, 128))
 MINOR = (((1,), (1,)), ((), ()))
 MAJOR = (((0,), (0,)), ((), ()))
 
@@ -28,8 +30,8 @@
     nz, ne,
     q_in, k_in, v_in, o_in, do_in, x_in, g_in, ids, route, gate_in, up_in, down_in,
     dq_out, dk_out, dv_out, dn_out,
-    W, KV, KT, Q, DO, OF, DOF, RDX, RD, PB, MJ, DKV, DQT, DQ, SB, RB, FB, XG, XS, XR, ACC, GU, RS, RR, MIX, OUT,
-    loc, sib_s, sib_r, wgt_s, wgt_r, wsb_s, wsb_r, kv_s, kv_r, gr_s, gr_r, tok_s, tok_r, ret_s, ret_r,
+    W, KV, KT, Q, DO, OF, DOF, RDX, RD, QT, DOT, PB, MJ, ST, DKV, DQT, DQ, SB, RB, FB, XG, XS, XR, ACC, GU, RSF, RSB, RRB, RR, MIX, OUT,
+    loc, sib_s, sib_r, own_s, own_r, wgt_s, wgt_r, wsb_s, wsb_r, kv_s, kv_r, gr_s, gr_r, tok_s, tok_r, ret_s, ret_r,
 ):
     half = nz // 2
     nk = 3 * half
@@ -110,9 +112,6 @@
         send(q_in.at[0, :, their_heads], Q.at[mine], sib_s.at[2], sib_r.at[2], sibling),
         send(do_in.at[0, :, their_heads], DO.at[mine], sib_s.at[3], sib_r.at[3], sibling),
     ]
-    for copy in swap:
-        copy.start()
-
     def kv_region(d, hop):
         at = plane(-hop if d == 0 else hop)
         return KV.at[at] if hop < half else KV.at[at, d]
@@ -135,34 +134,45 @@
 
     own = (gate_in, up_in, down_in)
 
-    def w_own(d, m):
-        return send(own[m].at[0], W.at[m, s], wgt_s.at[d, m], wgt_r.at[d, m], near[d])
+    def w_own(d, i):
+        m, first, rows = PIECES[i]
+        part = pl.ds(first, rows)
+        return send(own[m].at[0, part], W.at[m, s, part], own_s.at[d, i], own_r.at[d, i], near[d])
+
+    def w_start(i):
+        for d in range(2):
+            w_own(d, i).start()
 
     def w_own_sibling(m):
         return send(own[m].at[0], W.at[m, s], wsb_s.at[0, nk + m], wsb_r.at[0, nk + m], sibling)
 
     def w_region(d, k, core, rows_of=None):
-        hop = lax.div(k, 3) + 1
+        hop = k // 3 + 1
         at = plane(-hop if d == 0 else hop)
-        region = W.at[lax.rem(k, 3), 2 * at + core]
+        region = W.at[k % 3, 2 * at + core]
         if rows_of is None:
             return region
         rows = W.shape[2] // 2
         return region.at[pl.ds(rows * rows_of, rows)]
 
     def w_arrives(d, k, core):
-        last = not isinstance(k, jax.Array) and k >= nk - 3
+        last = k >= nk - 3
         return w_region(d, k, core, d if last else None)
 
     def w_leaves(d, k):
-        last = not isinstance(k, jax.Array) and k + 3 >= nk - 3
+        last = k + 3 >= nk - 3
         return w_region(d, k, c, d if last else None)
 
     def pump(k):
         for d in range(2):
             region = w_arrives(d, k, c)
-            arrived(region, wgt_r.at[d, k])
-            if isinstance(k, jax.Array) or k + 3 < nk:
+            if k < 3:
+                for i, (m, first, rows) in enumerate(PIECES):
+                    if m == k:
+                        arrived(region.at[pl.ds(first, rows)], own_r.at[d, i])
+            else:
+                arrived(region, wgt_r.at[d, k])
+            if k + 3 < nk:
                 leaving = w_leaves(d, k)
                 send(leaving, leaving, wgt_s.at[d, k + 3], wgt_r.at[d, k + 3], near[d]).start()
             send(region, region, wsb_s.at[d, k], wsb_r.at[d, k], sibling).start()
@@ -173,10 +183,13 @@
         slot = lax.bitwise_and(lane, SLOT - 1).astype(F32)
         named = jnp.zeros((TOK, ne * SLOT), F32)
         weight = jnp.zeros((TOK, ne * SLOT), F32)
-        for rank in range(ids.shape[2]):
-            hit = ids[0, :, rank : rank + 1] == expert
+        chosen = ids[0].astype(F32).T
+        shares = route[0].T
+        expert = expert.astype(F32)
+        for rank in range(chosen.shape[1]):
+            hit = chosen[:, rank : rank + 1] == expert
             named = jnp.where(hit, 1.0, named)
-            weight = jnp.where(hit, route[0, :, rank : rank + 1], weight)
+            weight = jnp.where(hit, shares[:, rank : rank + 1], weight)
         row = lax.broadcasted_iota(jnp.int32, (TOK, TOK), 0)
         col = lax.broadcasted_iota(jnp.int32, (TOK, TOK), 1)
         earlier = (col < row).astype(F32).astype(BF16)
@@ -207,14 +220,46 @@
 
         lax.fori_loop(lo, hi, body, 0)
 
+    swap[0].start()
+    swap[1].start()
+    w_start(0)
+    swap[2].start()
+    swap[3].start()
     local[0].wait()
     local[1].wait()
     arrived(KV.at[z, 0, theirs], sib_r.at[0])
     arrived(KV.at[z, 1, theirs], sib_r.at[1])
     for d in range(2):
         kv_forward(d, 0)
+    w_start(1)
     for m in range(3):
         w_own_sibling(m).start()
+
+    local[4].wait()
+    local[5].wait()
+    ones = jnp.ones((8, HEAD), BF16)
+
+    def head_dot(col):
+        cols = pl.ds(pl.multiple_of(col, HEAD), HEAD)
+        product = OF[:, cols].astype(F32) * DOF[:, cols].astype(F32)
+        high = product.astype(BF16)
+        low = (product - high.astype(F32)).astype(BF16)
+        return dot(ones, high, MINOR) + dot(ones, low, MINOR)
+
+    def their_dots(h):
+        RDX[h] = head_dot((other * groups + h) * HEAD)
+
+    def my_dots(h):
+        RD[h, :, mine] = head_dot((c * groups + h) * HEAD)
+
+    loop(0, groups, their_dots)
+    swap_dot = send(RDX, RD.at[:, :, mine], sib_s.at[4], sib_r.at[4], sibling)
+    swap_dot.start()
+    kv_step(1)
+    w_start(2)
+    loop(0, groups, my_dots)
+    kv_step(2)
+    w_start(3)
     local[2].wait()
     local[3].wait()
     select = routing()
@@ -222,63 +267,43 @@
         for n in range(model // 512):
             cols = pl.ds(512 * n, 512)
             XS[i, :, cols] = dot(select, XG[i, :, cols], MAJOR).astype(BF16)
-    loop(1, ne, lambda p: token_copy(p).start())
     my_slots = pl.ds(pl.multiple_of(e * SLOT, SLOT), SLOT)
     XR[:, my_slots, :] = XS[:, my_slots, :]
-    kv_step(1)
-    for d in range(2):
-        w_own(d, 0).start()
-
-    local[4].wait()
-    local[5].wait()
-    ones = jnp.ones((8, HEAD), BF16)
-
-    def head_dot(col):
-        cols = pl.ds(pl.multiple_of(col, HEAD), HEAD)
-        product = OF[:, cols].astype(F32) * DOF[:, cols].astype(F32)
-        high = product.astype(BF16)
-        low = (product - high.astype(F32)).astype(BF16)
-        return dot(ones, high, MINOR) + dot(ones, low, MINOR)
-
-    def both_dots(h):
-        RDX[h] = head_dot((other * groups + h) * HEAD)
-        RD[h, :, mine] = head_dot((c * groups + h) * HEAD)
-
-    loop(0, groups, both_dots)
-    swap_dot = send(RDX, RD.at[:, :, mine], sib_s.at[4], sib_r.at[4], sibling)
-    swap_dot.start()
-    kv_step(2)
-    for d in range(2):
-        w_own(d, 1).start()
-    DKV[...] = jnp.zeros(DKV.shape, F32)
     for hop in range(3, half):
         kv_step(hop)
-    for d in range(2):
-        w_own(d, 2).start()
+    w_start(4)
+    w_start(5)
+    DKV[...] = jnp.zeros(DKV.shape, F32)
+
+    def turn(j):
+        KT[j] = KV[j, 0].T
+
+    pump(0)
     if half > 2:
         kv_step(half)
-
-    def turn(j):
-        KT[j] = KV[j, 0].T
-
     loop(0, nz, turn)
     local[6].wait()
     local[7].wait()
     arrived(Q.at[theirs], sib_r.at[2])
     arrived(DO.at[theirs], sib_r.at[3])
     arrived(RD.at[:, :, theirs], sib_r.at[4])
-
-    in_loop = max(0, nk - 6)
-
-    def head(h):
-        cols = pl.ds(pl.multiple_of(h * HEAD, HEAD), HEAD)
-        queries = Q[:, cols]
-        grads = DO[:, cols]
-        dots = RD[h]
-
-        def scores(j, carry, diagonal):
-            top, total = carry
-            value = dot(KV[j, 0], queries, MINOR) * (scale * log2e)
+    pump(1)
+
+    pairs = groups // 2
+    last_pair = pairs - 1
+
+    def head_cols(pair, i):
+        return pl.ds(pl.multiple_of((2 * pair + i) * HEAD, HEAD), HEAD)
+
+    def flip(pair):
+        for i in range(2):
+            QT[i] = Q[:, head_cols(pair, i)].T
+
+    def scores(j, carry, into, diagonal):
+        out = []
+        for i in range(2):
+            top, total = carry[i]
+            value = dot(KV[j, 0], QT[i]) * (scale * log2e)
             if diagonal:
                 key = lax.broadcasted_iota(jnp.int32, (PAIR, PAIR), 0)
                 query = lax.broadcasted_iota(jnp.int32, (PAIR, PAIR), 1)
@@ -287,35 +312,80 @@
             new = jnp.maximum(top, jnp.max(value, axis=0))
             value = jnp.exp2(value - new[None])
             total = total * jnp.exp2(top - new) + jnp.sum(value, axis=0)
-            PB[j] = value.reshape(PAIR, PAIR)
-            MJ[j] = new
-            return new, total
-
-        carry = (jnp.full((8, PAIR), LOW, F32), jnp.zeros((8, PAIR), F32))
-        carry = lax.fori_loop(0, z, lambda j, x: scores(j, x, False), carry)
-        top, total = scores(z, carry, True)
-        peak = jnp.max(top, axis=0, keepdims=True)
-        total = jnp.sum(total * jnp.exp2(top - peak), axis=0, keepdims=True)
-        inverse = 1.0 / total
+            PB[i, j] = value.reshape(PAIR, PAIR)
+            MJ[into, i, j] = new
+            out.append((new, total))
+        return tuple(out)
+
+    def fresh():
+        return ((jnp.full((8, PAIR), LOW, F32), jnp.zeros((8, PAIR), F32)),) * 2
+
+    def settle(carry, into):
+        for i in range(2):
+            top, total = carry[i]
+            peak = jnp.max(top, axis=0, keepdims=True)
+            total = jnp.sum(total * jnp.exp2(top - peak), axis=0, keepdims=True)
+            ST[into, i, 0] = jnp.broadcast_to(peak, (8, PAIR))
+            ST[into, i, 1] = jnp.broadcast_to(1.0 / total, (8, PAIR))
+
+    def gradients(j, pair, into):
+        weights, lows = [], []
+        for i in range(2):
+            factor = jnp.exp2(MJ[into, i, j] - ST[into, i, 0]) * ST[into, i, 1]
+            weight = PB[i, j].reshape(PAIR // 8, 8, PAIR) * factor[None]
+            grad = dot(KV[j, 1], DOT[i]).reshape(PAIR // 8, 8, PAIR)
+            low = (weight * (grad - RD[2 * pair + i][None])).reshape(PAIR, PAIR).astype(BF16)
+            weights.append(weight.reshape(PAIR, PAIR).astype(BF16))
+            lows.append(low)
+            DQT[i] += dot(KT[j], low)
+        grads = jnp.concatenate([DO[:, head_cols(pair, i)] for i in range(2)], axis=0)
+        queries = jnp.concatenate([Q[:, head_cols(pair, i)] for i in range(2)], axis=0)
+        DKV[j, 1] += dot(jnp.concatenate(weights, axis=1), grads)
+        DKV[j, 0] += dot(jnp.concatenate(lows, axis=1), queries)
+
+    def begin(pair):
+        for i in range(2):
+            DOT[i] = DO[:, head_cols(pair, i)].T
         DQT[...] = jnp.zeros(DQT.shape, F32)
 
-        def gradients(j):
-            factor = jnp.exp2(MJ[j] - peak) * inverse
-            weights = PB[j].reshape(PAIR // 8, 8, PAIR) * factor[None]
-            grad = dot(KV[j, 1], grads, MINOR).reshape(PAIR // 8, 8, PAIR)
-            low = (weights * (grad - dots[None])).reshape(PAIR, PAIR).astype(BF16)
-            DKV[j, 1] += dot(weights.reshape(PAIR, PAIR).astype(BF16), grads)
-            DKV[j, 0] += dot(low, queries)
-            DQT[...] += dot(KT[j], low)
-
-        loop(0, z + 1, gradients)
-        DQ[:, cols] = (DQT[...] * scale).T.astype(BF16)
-
-        @pl.when((lax.rem(h, 2) == 1) & (lax.div(h, 2) < in_loop))
-        def _():
-            pump(lax.div(h, 2))
-
-    loop(0, groups, head)
+    def end(pair):
+        for i in range(2):
+            DQ[:, head_cols(pair, i)] = (DQT[i] * scale).T.astype(BF16)
+
+    def both(pair):
+        now = lax.rem(pair, 2)
+        flip(pair + 1)
+        begin(pair)
+
+        def step(j, carry, diagonal):
+            gradients(j, pair, now)
+            return scores(j, carry, 1 - now, diagonal)
+
+        carry = lax.fori_loop(0, z, lambda j, x: step(j, x, False), fresh())
+        settle(step(z, carry, True), 1 - now)
+        end(pair)
+        for at, k in schedule.items():
+
+            @pl.when(pair == at)
+            def _():
+                pump(k)
+
+        for i in (1, 2):
+
+            @pl.when(2 * pair + i < ne)
+            def _():
+                token_copy(2 * pair + i).start()
+
+    schedule = {0: 2, 2: 3, 3: 4, 4: 5, 5: 6} if nz == 8 else {0: 2}
+    in_loop = 2 + len(schedule)
+    flip(0)
+    carry = lax.fori_loop(0, z, lambda j, x: scores(j, x, 0, False), fresh())
+    settle(scores(z, carry, 0, True), 0)
+    loop(0, last_pair, both)
+    begin(last_pair)
+    loop(0, z + 1, lambda j: gradients(j, last_pair, last_pair % 2))
+    end(last_pair)
+    loop(2 * last_pair + 1, ne, lambda p: token_copy(p).start())
 
     dq_mine = pltpu.make_async_copy(DQ.at[mine], dq_out.at[0, :, my_heads], loc.at[11])
     dq_theirs = send(DQ.at[theirs], dq_out.at[0, :, my_heads], sib_s.at[5], sib_r.at[5], sibling)
@@ -378,36 +448,30 @@
             gather_wait(d, k)
         add(m, [plane(-hop), plane(hop)] if hop < half else [plane(hop)])
 
-    for k in range(in_loop, nk - 6):
-        pump(k)
     grad_step(half)
     loop(1, ne, token_arrived)
     for m in range(3):
         local[8 + m].wait()
         arrived(W.at[m, 2 * z + other], wsb_r.at[0, nk + m])
         add(m, [z], first=True)
-    rest = list(range(half - 1, 0, -1))
+    hops = [(hop, m) for hop in range(1, half + 1) for m in range(3)]
     done = 0
-    hops = [(hop, m) for hop in range(1, half + 1) for m in range(3)]
-    final = []
-    for step in range(nk - 6, nk):
-        if rest:
-            grad_step(rest.pop(0))
-            if not rest:
-                final = None
-        elif final is None:
-            final = grad_end()
-        while done < step:
+    for k in range(in_loop, nk):
+        pump(k)
+        if k == max(nk - 4, in_loop):
+            grad_step(half - 1)
+        if k == nk - 2 and half > 2:
+            grad_step(half - 2)
+        while done < k and (done < nk - 4 or k >= nk - 3):
             add_hop(*hops[done])
             done += 1
-            if done % 3 == 0:
+            if done % 3 == 0 and k < nk - 3:
                 break
-        pump(step)
-    if final is None:
-        final = grad_end()
     while done < nk:
         add_hop(*hops[done])
         done += 1
+    if half > 3:
+        grad_step(half - 3)
 
     rows = 16
 
@@ -421,37 +485,47 @@
     loop(0, ne * SLOT // rows, activate)
 
     parts = ret_s.shape[0]
-    span = model // parts
-
-    def ret_copy(i, p):
+    ready = [min(nz, -(-SLOT * (t + 1) // CAP)) for t in range(parts)]
+
+    def ret_copy(t, p):
         to = peer(p)
-        cols = pl.ds(span * i, span)
-        return send(
-            RS.at[pl.ds(pl.multiple_of(to * SLOT, SLOT), SLOT), cols],
-            RR.at[pl.ds(pl.multiple_of(e * SLOT, SLOT), SLOT), cols],
-            ret_s.at[i, p], ret_r.at[i, p], {"exp": to},
+        rows = pl.ds(SLOT * t, SLOT)
+        return send(RSB.at[to, rows], RRB.at[e, rows], ret_s.at[t, p], ret_r.at[t, p], {"exp": to})
+
+    def ret_arrived(t, p):
+        src = lax.rem(e - p + ne, ne)
+        arrived(RRB.at[src, pl.ds(SLOT * t, SLOT)], ret_r.at[t, p])
+
+    t = 0
+    for n in range(nz):
+        back = dot(GU[0], W[0, 2 * n : 2 * n + 2].reshape(PAIR, hid), MINOR) + dot(
+            GU[1], W[1, 2 * n : 2 * n + 2].reshape(PAIR, hid), MINOR
         )
-
-    def ret_arrived(i, p):
-        src = lax.rem(e - p + ne, ne)
-        arrived(RR.at[pl.ds(pl.multiple_of(src * SLOT, SLOT), SLOT), pl.ds(span * i, span)], ret_r.at[i, p])
-
-    for i in range(parts):
-        for n in range(i * span // PAIR, (i + 1) * span // PAIR):
-            back = dot(GU[0], W[0, 2 * n : 2 * n + 2].reshape(PAIR, hid), MINOR) + dot(
-                GU[1], W[1, 2 * n : 2 * n + 2].reshape(PAIR, hid), MINOR
-            )
-            RS[:, PAIR * n : PAIR * n + PAIR] = back.astype(BF16)
-        loop(1, ne, lambda p: ret_copy(i, p).start())
-        cols = pl.ds(span * i, span)
-        RR[my_slots, cols] = RS[my_slots, cols]
+        for p in range(ne):
+            RSF[p, CAP * n : CAP * n + SLOT, :] = back[SLOT * p : SLOT * p + SLOT]
+        while t < parts and ready[t] == n + 1:
+            rows = pl.ds(SLOT * t, SLOT)
+            RSB[:, rows, :] = RSF[:, rows, :].astype(BF16)
+            loop(1, ne, lambda p: ret_copy(t, p).start())
+            RRB[e, rows, :] = RSB[e, rows, :]
+            t += 1
+    final = grad_end()
     outs = []
-    for i in range(parts):
-        loop(1, ne, lambda p: ret_arrived(i, p))
-        cols = pl.ds(span * i, span)
-        back = RR[:, cols]
+    row = lax.broadcasted_iota(jnp.int32, (SLOT, PAIR), 0)
+    t = 0
+    for n in range(nz):
+        while t < parts and SLOT * t < CAP * (n + 1):
+            loop(1, ne, lambda p: ret_arrived(t, p))
+            rows = pl.ds(SLOT * t, SLOT)
+            RSF[:, rows, :] = RRB[:, rows, :].astype(F32)
+            t += 1
+        for p in range(ne):
+            slots = RSF[p, CAP * n : CAP * n + SLOT, :]
+            RR[SLOT * p : SLOT * p + SLOT, :] = jnp.where(row < CAP, slots, 0.0).astype(BF16)
+        back = RR[...]
+        cols = pl.ds(PAIR * n, PAIR)
         OUT[:, cols] = (dot(MIX[0], back) + dot(MIX[1], back)).astype(BF16)
-        copy = pltpu.make_async_copy(OUT.at[:, cols], dn_out.at[0, :, cols], loc.at[14 + i])
+        copy = pltpu.make_async_copy(OUT.at[:, cols], dn_out.at[0, :, cols], loc.at[14 + n])
         copy.start()
         outs.append(copy)
 
@@ -461,8 +535,8 @@
     for d in range(2):
         for hop in range(half):
             kv_sent(d, hop)
-        for m in range(3):
-            w_own(d, m).wait_send()
+        for i in range(len(PIECES)):
+            w_own(d, i).wait_send()
         for k in range(nk - 3):
             sent(w_leaves(d, k), wgt_s.at[d, k + 3])
         for k in range(nk):
@@ -472,8 +546,8 @@
     for m in range(3):
         w_own_sibling(m).wait_send()
     loop(1, ne, lambda p: token_copy(p).wait_send())
-    for i in range(parts):
-        loop(1, ne, lambda p: ret_copy(i, p).wait_send())
+    for t in range(parts):
+        loop(1, ne, lambda p: ret_copy(t, p).wait_send())
     dq_mine.wait()
     dq_theirs.wait_send()
     arrived(dq_out.at[0, :, their_heads], sib_r.at[5])
@@ -494,7 +568,7 @@
     model = normed.shape[2]
     rows, hid = gate_w.shape[1:]
     slots = ne * SLOT
-    parts = 4
+    parts = -(-CAP * nz // SLOT)
     dma = pltpu.SemaphoreType.DMA
     anywhere = pl.BlockSpec(memory_space=pl.ANY)
     vmem = pl.BlockSpec(memory_space=pltpu.VMEM)
@@ -508,10 +582,13 @@
         pltpu.VMEM((TOK, heads), BF16),
         pltpu.VMEM((groups, 8, TOK), F32),
         pltpu.VMEM((groups, 8, PAIR), F32),
-        pltpu.VMEM((nz, PAIR, PAIR), F32),
-        pltpu.VMEM((nz, 8, PAIR), F32),
+        pltpu.VMEM((2, HEAD, PAIR), BF16),
+        pltpu.VMEM((2, HEAD, PAIR), BF16),
+        pltpu.VMEM((2, nz, PAIR, PAIR), F32),
+        pltpu.VMEM((2, 2, nz, 8, PAIR), F32),
+        pltpu.VMEM((2, 2, 2, 8, PAIR), F32),
         pltpu.VMEM((nz, 2, PAIR, HEAD), F32),
-        pltpu.VMEM((HEAD, PAIR), F32),
+        pltpu.VMEM((2, HEAD, PAIR), F32),
         pltpu.VMEM((PAIR, width), BF16),
         pltpu.VMEM((2, half, 2, PAIR, HEAD), BF16),
         pltpu.VMEM((2, half, 2, PAIR, HEAD), BF16),
@@ -521,12 +598,15 @@
         pltpu.VMEM((2, slots, model), BF16),
         pltpu.VMEM((3, slots, hid), F32),
         pltpu.VMEM((2, slots, hid), BF16),
-        pltpu.VMEM((slots, model), BF16),
-        pltpu.VMEM((slots, model), BF16),
+        pltpu.VMEM((ne, SLOT * parts + 8, PAIR), F32),
+        pltpu.VMEM((ne, SLOT * parts, PAIR), BF16),
+        pltpu.VMEM((ne, SLOT * parts, PAIR), BF16),
+        pltpu.VMEM((slots, PAIR), BF16),
         pltpu.VMEM((2, TOK, slots), BF16),
         pltpu.VMEM((TOK, model), BF16),
-        dma((14 + parts,)),
+        dma((14 + nz,)),
         dma((8,)), dma((8,)),
+        dma((2, len(PIECES))), dma((2, len(PIECES))),
         dma((2, nk)), dma((2, nk)),
         dma((2, nk + 3)), dma((2, nk + 3)),
         dma((2, half)), dma((2, half)),
@@ -546,10 +626,10 @@
         out_specs=[anywhere] * 4,
         scratch_shapes=scratch,
         compiler_params=pltpu.CompilerParams(
-            collective_id=0, has_side_effects=True, vmem_limit_bytes=60 * 1024 * 1024
+            collective_id=0, has_side_effects=True, vmem_limit_bytes=62 * 1024 * 1024
         ),
         name="layer_backward",
-    )(queries, keys, values, attn_out, d_attn, normed, d_moe, ids, route, gate_w, up_w, down_t)
+    )(queries, keys, values, attn_out, d_attn, normed, d_moe, jnp.swapaxes(ids, 1, 2), jnp.swapaxes(route, 1, 2), gate_w, up_w, down_t)
 
 
 def solution(mesh):

time: 185 us -> 144 us (0.78)
  Pallas kernels: 177 us -> 138 us
  local copies, waits for them, and re-layouts: 6.79 us -> 4.64 us
    pallas_call x1, Pallas kernels: 177 us -> 138 us  [local(): pl.pallas_call(functools.partial(kernel, nz, ne), out_shape=(jax.ShapeDty...]
    unnamed x14 -> x10, local copies, waits for them, and re-layouts: 6.79 us -> 4.64 us
where the time goes in v2:
time: 144 us
  Pallas kernels  138 us (96%)
  local copies, waits for them, and re-layouts  4.64 us (3%)
    pallas_call x1, Pallas kernels, local(): pl.pallas_call(functools.partial(kernel, nz, ne), out_shape=(jax.ShapeDty...  138 us
    unnamed x10, local copies, waits for them, and re-layouts  4.64 us

profile of v2, /device:TPU:1, one launch (start us, length us, event | category | flops | bytes accessed | tf_op | source)
XLA Modules:
  0.0 143.6 jit_solution(11553026744036106298)
XLA Ops:
  0.6 138.3 %layer_backward.1 = (bf16[1,128,4096]{2,1,0:T(8,128)(2,1)}, bf16[1,128,256]{2,1,0:T(8,128)(2,1)}, bf16[1,128,256]{2,1,0:T(8,128)(2,1)}, bf16[1,128,2048]{2,1,0:T(8,128)(2,1)}) custom-call(bf16[1,128,4096]{2,1,0:T(8,128)(2,1)} %q_in.1, bf16[1,128,256]{2,1,0:T(8,128)(2,1)} %k_in.1, bf16[1,128,256]{2,1,0:T(8,128)(2,1)} %v_in.1, bf16[1,128,4096]{2,1,0:T(8,128)(2,1)} %o_in.1, ...), custom_call_target="tpu_custom_call" | custom-call | tf_op jit(solution)/shard_map/layer_backward/pallas_call | solution.py:617
  139.0 0.0 copy-start.2
  139.0 0.0 copy-start
  139.0 2.3 %copy.20 = bf16[1,128,4096]{2,1,0:T(8,128)(2,1)} copy(bf16[1,128,4096]{2,1,0:T(8,128)(2,1)} %get-tuple-element.8) | data formatting | bytes 2097152
  141.3 0.0 copy-done.2
  141.3 0.0 copy-start.1
  141.3 0.6 copy.21
  142.0 0.2 copy-done.1
  142.2 0.6 copy.22
  142.8 0.0 copy-done
  142.8 0.8 copy.23
Async XLA Ops:
  139.0 2.4 %copy-start.2 = (bf16[1,128,256]{2,1,0:T(8,128)(2,1)S(1)}, bf16[1,128,256]{2,1,0:T(8,128)(2,1)}, u32[]{:S(2)}) copy-start(bf16[1,128,256]{2,1,0:T(8,128)(2,1)} %get-tuple-element.9) | copy-start | bytes 196612
  139.0 3.9 %copy-start = (bf16[1,128,2048]{2,1,0:T(8,128)(2,1)S(1)}, bf16[1,128,2048]{2,1,0:T(8,128)(2,1)}, u32[]{:S(2)}) copy-start(bf16[1,128,2048]{2,1,0:T(8,128)(2,1)} %get-tuple-element.11) | copy-start | bytes 1572868
  141.3 0.9 copy-start.1

commit v3 on v2

--- a/solution.py
+++ b/solution.py
@@ -92,7 +92,7 @@
         (down_in.at[0], W.at[2, s]),
     ]
     local = [pltpu.make_async_copy(a, b, loc.at[i]) for i, (a, b) in enumerate(local)]
-    for copy in local:
+    for copy in local[:2]:
         copy.start()
 
     barrier = pltpu.get_barrier_semaphore()
@@ -223,8 +223,6 @@
     swap[0].start()
     swap[1].start()
     w_start(0)
-    swap[2].start()
-    swap[3].start()
     local[0].wait()
     local[1].wait()
     arrived(KV.at[z, 0, theirs], sib_r.at[0])
@@ -232,6 +230,10 @@
     for d in range(2):
         kv_forward(d, 0)
     w_start(1)
+    for copy in local[2:]:
+        copy.start()
+    swap[2].start()
+    swap[3].start()
     for m in range(3):
         w_own_sibling(m).start()
 
@@ -456,12 +458,24 @@
         add(m, [z], first=True)
     hops = [(hop, m) for hop in range(1, half + 1) for m in range(3)]
     done = 0
+    rows = 16
+
+    def prepare(i):
+        at = pl.ds(pl.multiple_of(i * rows, rows), rows)
+        gate, up = ACC[0, at, :], ACC[1, at, :]
+        sig = 1.0 / (1.0 + jnp.exp(-gate))
+        ACC[0, at, :] = up * sig * (1.0 + gate * (1.0 - sig))
+        ACC[1, at, :] = gate * sig
+
     for k in range(in_loop, nk):
+        if k == nk - 1:
+            while done < k:
+                add_hop(*hops[done])
+                done += 1
+            loop(0, ne * SLOT // rows, prepare)
         pump(k)
-        if k == max(nk - 4, in_loop):
+        if k == nk - 1:
             grad_step(half - 1)
-        if k == nk - 2 and half > 2:
-            grad_step(half - 2)
         while done < k and (done < nk - 4 or k >= nk - 3):
             add_hop(*hops[done])
             done += 1
@@ -470,31 +484,33 @@
     while done < nk:
         add_hop(*hops[done])
         done += 1
-    if half > 3:
-        grad_step(half - 3)
-
-    rows = 16
+    if half > 2:
+        grad_step(half - 2)
 
     def activate(i):
         at = pl.ds(pl.multiple_of(i * rows, rows), rows)
-        gate, up, grad = ACC[0, at, :], ACC[1, at, :], ACC[2, at, :]
-        sig = 1.0 / (1.0 + jnp.exp(-gate))
-        GU[0, at, :] = (grad * up * sig * (1.0 + gate * (1.0 - sig))).astype(BF16)
-        GU[1, at, :] = (grad * (gate * sig)).astype(BF16)
+        grad = ACC[2, at, :]
+        GU[0, at, :] = (grad * ACC[0, at, :]).astype(BF16)
+        GU[1, at, :] = (grad * ACC[1, at, :]).astype(BF16)
 
     loop(0, ne * SLOT // rows, activate)
 
     parts = ret_s.shape[0]
-    ready = [min(nz, -(-SLOT * (t + 1) // CAP)) for t in range(parts)]
+    tiles = RSB.shape[1] // SLOT
+    first = [2 * t for t in range(parts)] + [tiles]
+    ready = [min(nz, -(-SLOT * first[t + 1] // CAP)) for t in range(parts)]
+
+    def ret_rows(t):
+        return pl.ds(SLOT * first[t], SLOT * (first[t + 1] - first[t]))
 
     def ret_copy(t, p):
         to = peer(p)
-        rows = pl.ds(SLOT * t, SLOT)
+        rows = ret_rows(t)
         return send(RSB.at[to, rows], RRB.at[e, rows], ret_s.at[t, p], ret_r.at[t, p], {"exp": to})
 
     def ret_arrived(t, p):
         src = lax.rem(e - p + ne, ne)
-        arrived(RRB.at[src, pl.ds(SLOT * t, SLOT)], ret_r.at[t, p])
+        arrived(RRB.at[src, ret_rows(t)], ret_r.at[t, p])
 
     t = 0
     for n in range(nz):
@@ -503,8 +519,10 @@
         )
         for p in range(ne):
             RSF[p, CAP * n : CAP * n + SLOT, :] = back[SLOT * p : SLOT * p + SLOT]
+        if n == 4 and half > 3:
+            grad_step(half - 3)
         while t < parts and ready[t] == n + 1:
-            rows = pl.ds(SLOT * t, SLOT)
+            rows = ret_rows(t)
             RSB[:, rows, :] = RSF[:, rows, :].astype(BF16)
             loop(1, ne, lambda p: ret_copy(t, p).start())
             RRB[e, rows, :] = RSB[e, rows, :]
@@ -514,9 +532,9 @@
     row = lax.broadcasted_iota(jnp.int32, (SLOT, PAIR), 0)
     t = 0
     for n in range(nz):
-        while t < parts and SLOT * t < CAP * (n + 1):
+        while t < parts and SLOT * first[t] < CAP * (n + 1):
             loop(1, ne, lambda p: ret_arrived(t, p))
-            rows = pl.ds(SLOT * t, SLOT)
+            rows = ret_rows(t)
             RSF[:, rows, :] = RRB[:, rows, :].astype(F32)
             t += 1
         for p in range(ne):
@@ -559,6 +577,11 @@
         copy.wait()
 
 
+def hand_over(*refs):
+    for src, dst in zip(refs[:4], refs[4:]):
+        dst[...] = src[...]
+
+
 def local(nz, ne, queries, keys, values, attn_out, d_attn, normed, d_moe, ids, route, gate_w, up_w, down_t):
     half = nz // 2
     nk = 3 * half
@@ -568,7 +591,8 @@
     model = normed.shape[2]
     rows, hid = gate_w.shape[1:]
     slots = ne * SLOT
-    parts = -(-CAP * nz // SLOT)
+    tiles = -(-CAP * nz // SLOT)
+    parts = -(-tiles // 2)
     dma = pltpu.SemaphoreType.DMA
     anywhere = pl.BlockSpec(memory_space=pl.ANY)
     vmem = pl.BlockSpec(memory_space=pltpu.VMEM)
@@ -598,9 +622,9 @@
         pltpu.VMEM((2, slots, model), BF16),
         pltpu.VMEM((3, slots, hid), F32),
         pltpu.VMEM((2, slots, hid), BF16),
-        pltpu.VMEM((ne, SLOT * parts + 8, PAIR), F32),
-        pltpu.VMEM((ne, SLOT * parts, PAIR), BF16),
-        pltpu.VMEM((ne, SLOT * parts, PAIR), BF16),
+        pltpu.VMEM((ne, SLOT * tiles + 8, PAIR), F32),
+        pltpu.VMEM((ne, SLOT * tiles, PAIR), BF16),
+        pltpu.VMEM((ne, SLOT * tiles, PAIR), BF16),
         pltpu.VMEM((slots, PAIR), BF16),
         pltpu.VMEM((2, TOK, slots), BF16),
         pltpu.VMEM((TOK, model), BF16),
@@ -614,7 +638,7 @@
         dma((ne,)), dma((ne,)),
         dma((parts, ne)), dma((parts, ne)),
     ]
-    return pl.pallas_call(
+    results = pl.pallas_call(
         functools.partial(kernel, nz, ne),
         out_shape=(
             jax.ShapeDtypeStruct(queries.shape, BF16),
@@ -630,6 +654,13 @@
         ),
         name="layer_backward",
     )(queries, keys, values, attn_out, d_attn, normed, d_moe, jnp.swapaxes(ids, 1, 2), jnp.swapaxes(route, 1, 2), gate_w, up_w, down_t)
+    return pl.pallas_call(
+        hand_over,
+        out_shape=tuple(jax.ShapeDtypeStruct(r.shape, BF16) for r in results),
+        in_specs=[vmem] * 4,
+        out_specs=[vmem] * 4,
+        name="hand_over",
+    )(*results)
 
 
 def solution(mesh):

time: 144 us -> 141 us (0.979)
  local copies, waits for them, and re-layouts: 4.64 us -> 0 us
  Pallas kernels: 138 us -> 140 us
    unnamed x10 -> x0, local copies, waits for them, and re-layouts: 4.64 us -> none
    pallas_call x0 -> x1, Pallas kernels: none -> 2.65 us  [local(): pl.pallas_call(hand_over, out_shape=tuple((jax.ShapeDtypeStruct(r.shape,...]
where the time goes in v3:
time: 141 us
  Pallas kernels  140 us (99%)
    pallas_call x1, Pallas kernels, local(): pl.pallas_call(functools.partial(kernel, nz, ne), out_shape=(jax.ShapeDty...  137 us

profile of v3, /device:TPU:1, one launch (start us, length us, event | category | flops | bytes accessed | tf_op | source)
XLA Modules:
  0.0 140.7 jit_solution(6998569603824946460)
XLA Ops:
  0.6 137.4 %layer_backward.1 = (bf16[1,128,4096]{2,1,0:T(8,128)(2,1)}, bf16[1,128,256]{2,1,0:T(8,128)(2,1)}, bf16[1,128,256]{2,1,0:T(8,128)(2,1)}, bf16[1,128,2048]{2,1,0:T(8,128)(2,1)}) custom-call(bf16[1,128,4096]{2,1,0:T(8,128)(2,1)} %q_in.1, bf16[1,128,256]{2,1,0:T(8,128)(2,1)} %k_in.1, bf16[1,128,256]{2,1,0:T(8,128)(2,1)} %v_in.1, bf16[1,128,4096]{2,1,0:T(8,128)(2,1)} %o_in.1, ...), custom_call_target="tpu_custom_call" | custom-call | tf_op jit(solution)/shard_map/layer_backward/pallas_call | solution.py:641
  138.1 2.7 %hand_over.1 = (bf16[1,128,4096]{2,1,0:T(8,128)(2,1)}, bf16[1,128,256]{2,1,0:T(8,128)(2,1)}, bf16[1,128,256]{2,1,0:T(8,128)(2,1)}, bf16[1,128,2048]{2,1,0:T(8,128)(2,1)}) custom-call(bf16[1,128,4096]{2,1,0:T(8,128)(2,1)} %get-tuple-element.8.refs_0_, bf16[1,128,256]{2,1,0:T(8,128)(2,1)} %get-tuple-element.9.refs_1_, ...), custom_call_target="tpu_custom_call" | custom-call | tf_op jit(solution)/shard_map/hand_over/pallas_call | solution.py:657

commit v4 on v3

--- a/solution.py
+++ b/solution.py
@@ -384,6 +384,7 @@
     carry = lax.fori_loop(0, z, lambda j, x: scores(j, x, 0, False), fresh())
     settle(scores(z, carry, 0, True), 0)
     loop(0, last_pair, both)
+    pump(in_loop)
     begin(last_pair)
     loop(0, z + 1, lambda j: gradients(j, last_pair, last_pair % 2))
     end(last_pair)
@@ -467,7 +468,7 @@
         ACC[0, at, :] = up * sig * (1.0 + gate * (1.0 - sig))
         ACC[1, at, :] = gate * sig
 
-    for k in range(in_loop, nk):
+    for k in range(in_loop + 1, nk):
         if k == nk - 1:
             while done < k:
                 add_hop(*hops[done])
@@ -524,7 +525,8 @@
         while t < parts and ready[t] == n + 1:
             rows = ret_rows(t)
             RSB[:, rows, :] = RSF[:, rows, :].astype(BF16)
-            loop(1, ne, lambda p: ret_copy(t, p).start())
+            for p in sorted(range(1, ne), key=lambda p: (p % 4 != 2) + (p // 4 != 2)):
+                ret_copy(t, p).start()
             RRB[e, rows, :] = RSB[e, rows, :]
             t += 1
     final = grad_end()

time: 141 us -> 141 us (level)
  no operation moved by 1% of the time
where the time goes in v4:
time: 141 us; the launch traced here: 140 us
  Pallas kernels  140 us (99%)
    pallas_call x1, Pallas kernels, local(): pl.pallas_call(functools.partial(kernel, nz, ne), out_shape=(jax.ShapeDty...  137 us

profile of v4, /device:TPU:1, one launch (start us, length us, event | category | flops | bytes accessed | tf_op | source)
XLA Modules:
  0.0 140.4 jit_solution(8236508089051652986)
XLA Ops:
  0.6 137.1 %layer_backward.1 = (bf16[1,128,4096]{2,1,0:T(8,128)(2,1)}, bf16[1,128,256]{2,1,0:T(8,128)(2,1)}, bf16[1,128,256]{2,1,0:T(8,128)(2,1)}, bf16[1,128,2048]{2,1,0:T(8,128)(2,1)}) custom-call(bf16[1,128,4096]{2,1,0:T(8,128)(2,1)} %q_in.1, bf16[1,128,256]{2,1,0:T(8,128)(2,1)} %k_in.1, bf16[1,128,256]{2,1,0:T(8,128)(2,1)} %v_in.1, bf16[1,128,4096]{2,1,0:T(8,128)(2,1)} %o_in.1, ...), custom_call_target="tpu_custom_call" | custom-call | tf_op jit(solution)/shard_map/layer_backward/pallas_call | solution.py:643
  137.8 2.7 %hand_over.1 = (bf16[1,128,4096]{2,1,0:T(8,128)(2,1)}, bf16[1,128,256]{2,1,0:T(8,128)(2,1)}, bf16[1,128,256]{2,1,0:T(8,128)(2,1)}, bf16[1,128,2048]{2,1,0:T(8,128)(2,1)}) custom-call(bf16[1,128,4096]{2,1,0:T(8,128)(2,1)} %get-tuple-element.8.refs_0_, bf16[1,128,256]{2,1,0:T(8,128)(2,1)} %get-tuple-element.9.refs_1_, ...), custom_call_target="tpu_custom_call" | custom-call | tf_op jit(solution)/shard_map/hand_over/pallas_call | solution.py:659
